TPU v7x, 512 devices: a whole 4x4x16 slice. The times are simulated.
512 devices in a mesh: gx: 16 (over z_hi, y), gy: 4 (over z_lo), gz: 8 (over x, core).
Axes of the slice: x: 4, y: 4, z: 16 (z_hi: 4, z_lo: 4; z = z_hi * 4 + z_lo), core: 2. Of those that a mesh axis runs over, the one named last changes fastest.
Arguments:
- initial_state: float32 [64, 32, 1024], P('gx', 'gy', 'gz'), may hold values from -6 to 6
- conductivity: float32 [64, 32, 1024], P('gx', 'gy', 'gz'), may hold values from 0.3 to 3
- reaction: float32 [64, 32, 1024], P('gx', 'gy', 'gz'), may hold values from 0.02 to 0.2
- source: float32 [64, 32, 1024], P('gx', 'gy', 'gz'), may hold values from -12 to 12, as said below
Outputs:
- solution: float32 [64, 32, 1024], P('gx', 'gy', 'gz')
- final_residual: float32 [64, 32, 1024], P('gx', 'gy', 'gz')
Inputs may be any that keep to these rules, and one draw needn't show every extreme that they name: Real-valued source of order one.
All inputs are finite; a program needn't handle non-finite values.
Results may differ from a plain program's by a relative error of at most 0.0003.
Values sent between devices are 32-bit elements; how exact they have to be, the bound alone decides.
A program may use at most 64 MiB of HBM per device.

v0:
```python
import jax
import jax.numpy as jnp
from jax import lax
from jax.sharding import PartitionSpec as P

NEWTON = 2
KRYLOV = 3


EPS_SQUARE = 0.25


def padded_2(block, sides, width):
    for axis, dim in sides:
        count = lax.axis_size(axis)
        forward = [(i, i + 1) for i in range(count - 1)]
        forward.append((count - 1, 0))
        backward = [(target, source) for source, target in forward]
        low = lax.ppermute(
            lax.slice_in_dim(block, block.shape[dim] - width, None, axis=dim), axis, forward
        )
        high = lax.ppermute(lax.slice_in_dim(block, 0, width, axis=dim), axis, backward)
        block = jnp.concatenate([low, block, high], axis=dim)
    return block


def face_set(lower_u, lower_k, upper_u, upper_k):
    mean_k = 2.0 * lower_k * upper_k / (lower_k + upper_k)
    difference = upper_u - lower_u
    root_term = jnp.sqrt(EPS_SQUARE + difference * difference)
    return (
        mean_k * root_term * difference,
        mean_k * (EPS_SQUARE + 2.0 * difference * difference) / root_term,
    )


def restrict(field):
    first, second, third = field.shape
    return field.reshape(first // 2, 2, second // 2, 2, third // 2, 2).sum(axis=(1, 3, 5))


def prolong(field):
    return jnp.repeat(jnp.repeat(jnp.repeat(field, 2, 0), 2, 1), 2, 2)


def parity(array_shape, axis_no, odd_flag):
    marks = (jnp.arange(array_shape[axis_no]) % 2 == odd_flag).astype(jnp.float32)
    layout = [1, 1, 1]
    layout[axis_no] = array_shape[axis_no]
    return marks.reshape(layout)


def cut(array, axis_no, start, stop):
    slices = [slice(1, -1), slice(1, -1), slice(1, -1)]
    slices[axis_no] = slice(start, stop)
    return array[tuple(slices)]


def padded_sides(padded):
    upper_side, lower_side = ([], [])
    for axis_no in range(3):
        length = padded.shape[axis_no] - 2
        upper_side.append(cut(padded, axis_no, 2, length + 2))
        lower_side.append(cut(padded, axis_no, 0, length))
    return (upper_side, lower_side)


def fine_sides(field):
    return padded_sides(padded_2(field, (("gx", 0), ("gy", 1), ("gz", 2)), 1))


def image_sides(field):
    return padded_sides(padded_2(field, (("gx", 0), ("gy", 1), ("gz", 2)), 1))


def coarse_sides(field):
    return padded_sides(padded_2(field, (("gx", 0), ("gy", 1), ("gz", 2)), 1))


def apply_op(field, react_field, w_up, w_lo, sides):
    upper_side, lower_side = sides(field)
    result = react_field * field
    for axis_no in range(3):
        result = (
            result
            + w_up[axis_no] * (field - upper_side[axis_no])
            + w_lo[axis_no] * (field - lower_side[axis_no])
        )
    return result


def diagonal_of(react_field, w_up, w_lo):
    diagonal = react_field
    for axis_no in range(3):
        diagonal = diagonal + w_up[axis_no] + w_lo[axis_no]
    return diagonal


def smooth(rhs_field, react_field, w_up, w_lo, sides, low_end):
    inverse = 1.0 / diagonal_of(react_field, w_up, w_lo)
    centre = (2.0 + low_end) / 2.0
    half_width = (2.0 - low_end) / 2.0
    sigma_ratio = centre / half_width
    rho_now = 1.0 / sigma_ratio
    update = inverse * rhs_field * (1.0 / centre)
    result = update
    remain = rhs_field
    remain = remain - apply_op(update, react_field, w_up, w_lo, sides)
    rho_new = 1.0 / (2.0 * sigma_ratio - rho_now)
    update = rho_new * rho_now * update + 2.0 * rho_new / half_width * (inverse * remain)
    result = result + update
    return result


def coefficients(state, conductivity, reaction, source):
    padded = padded_2(jnp.stack([state, conductivity]), (("gx", 1), ("gy", 2), ("gz", 3)), 1)
    padded_u = padded[0]
    padded_k = padded[1]
    w_up, w_lo, flux_up, flux_lo = ([], [], [], [])
    for axis_no in range(3):
        length = state.shape[axis_no]
        flux, weight = face_set(
            cut(padded_u, axis_no, 0, length + 1),
            cut(padded_k, axis_no, 0, length + 1),
            cut(padded_u, axis_no, 1, length + 2),
            cut(padded_k, axis_no, 1, length + 2),
        )
        w_up.append(lax.slice_in_dim(weight, 1, length + 1, axis=axis_no))
        w_lo.append(lax.slice_in_dim(weight, 0, length, axis=axis_no))
        flux_up.append(lax.slice_in_dim(flux, 1, length + 1, axis=axis_no))
        flux_lo.append(lax.slice_in_dim(flux, 0, length, axis=axis_no))
    residual = reaction * state
    for axis_no in range(3):
        residual = residual - (flux_up[axis_no] - flux_lo[axis_no])
    residual = residual - source
    return (w_up, w_lo, residual)


def precond_sum(remain, zed):
    return lax.psum(jnp.sum(remain * zed), ("gx", "gy", "gz"))


def local(initial_state, conductivity, reaction, source):
    state = initial_state
    for newton_no in range(NEWTON):
        w_up, w_lo, residual = coefficients(state, conductivity, reaction, source)
        react_coarse = restrict(reaction)
        wc_up = [restrict(w_up[axis_no] * parity(state.shape, axis_no, 1)) for axis_no in range(3)]
        wc_lo = [restrict(w_lo[axis_no] * parity(state.shape, axis_no, 0)) for axis_no in range(3)]

        def precondition(remain):
            fine = smooth(remain, reaction, w_up, w_lo, fine_sides, 0.3)
            coarse = smooth(restrict(remain), react_coarse, wc_up, wc_lo, coarse_sides, 0.05)
            return fine + prolong(coarse)

        remain = -residual
        delta_sol = jnp.zeros_like(state)
        zed = precondition(remain)
        search = zed
        rz_now = precond_sum(remain, zed)
        for step_no in range(KRYLOV):
            image = apply_op(search, reaction, w_up, w_lo, image_sides)
            alpha = rz_now / lax.psum(jnp.sum(search * image), ("gx", "gy", "gz"))
            delta_sol = delta_sol + alpha * search
            remain = remain - alpha * image
            if step_no + 1 < KRYLOV:
                zed = precondition(remain)
                rz_new = precond_sum(remain, zed)
                search = zed + rz_new / rz_now * search
                rz_now = rz_new
        state = state + delta_sol
    w_up, w_lo, residual = coefficients(state, conductivity, reaction, source)
    return (state, residual)


def solution(mesh):
    placed = (P("gx", "gy", "gz"), P("gx", "gy", "gz"), P("gx", "gy", "gz"), P("gx", "gy", "gz"))
    return jax.shard_map(
        local,
        mesh=mesh,
        in_specs=placed,
        out_specs=(P("gx", "gy", "gz"), P("gx", "gy", "gz")),
        check_vma=False,
    )
```

profile of v0, /device:TPU:1, one launch (start us, length us, event | category | flops | bytes accessed | tf_op | source)
XLA Modules:
  0.0 1645.2 jit_solution(12575031405306118716)
XLA Ops:
  1.4 15.7 collective-permute-start.1
  19.1 8.5 collective-permute-done
  105.2 8.4 collective-permute-done.19
  130.0 103.2 %all-reduce.1 = (f32[]{:T(128)}, f32[]{:T(128)}) all-reduce(f32[]{:T(128)} %get-tuple-element.13, f32[]{:T(128)} %get-tuple-element.12), channel_id=1, replica_groups=mesh['gx'=16,'gy'=4,'gz'=8] {'gx','gy','gz'}, use_global_device_ids=true, to_apply=%region_9.10 | all-reduce | flops 2 | bytes 16 | tf_op jit(solution)/shard_map/psum | solution.py:140
  242.7 8.4 collective-permute-done.31
  284.1 103.0 %psum.86 = f32[]{:T(128)} all-reduce(f32[]{:T(128)} %get-tuple-element.40), channel_id=1, replica_groups=mesh['gx'=16,'gy'=4,'gz'=8] {'gx','gy','gz'}, use_global_device_ids=true, to_apply=%region_14.15 | all-reduce | flops 1 | bytes 8 | tf_op jit(solution)/shard_map/psum | solution.py:140
  397.9 8.4 collective-permute-done.37
  419.5 103.1 %psum.87 = f32[]{:T(128)} all-reduce(f32[]{:T(128)} %get-tuple-element.38), channel_id=1, replica_groups=mesh['gx'=16,'gy'=4,'gz'=8] {'gx','gy','gz'}, use_global_device_ids=true, to_apply=%region_16.17 | all-reduce | flops 1 | bytes 8 | tf_op jit(solution)/shard_map/psum | solution.py:163
  532.2 8.4 collective-permute-done.49
  573.4 102.9 %psum.88 = f32[]{:T(128)} all-reduce(f32[]{:T(128)} %get-tuple-element.34), channel_id=1, replica_groups=mesh['gx'=16,'gy'=4,'gz'=8] {'gx','gy','gz'}, use_global_device_ids=true, to_apply=%region_19.20 | all-reduce | flops 1 | bytes 8 | tf_op jit(solution)/shard_map/psum | solution.py:140
  687.0 8.4 collective-permute-done.55
  708.6 103.1 %psum.89 = f32[]{:T(128)} all-reduce(f32[]{:T(128)} %fusion.143), channel_id=1, replica_groups=mesh['gx'=16,'gy'=4,'gz'=8] {'gx','gy','gz'}, use_global_device_ids=true, to_apply=%region_21.22 | all-reduce | flops 1 | bytes 8 | tf_op jit(solution)/shard_map/psum | solution.py:163
  820.2 8.5 collective-permute-done.60
  905.8 8.4 collective-permute-done.79
  930.6 102.9 %all-reduce = (f32[]{:T(128)}, f32[]{:T(128)}) all-reduce(f32[]{:T(128)} %get-tuple-element.11, f32[]{:T(128)} %get-tuple-element.10), channel_id=1, replica_groups=mesh['gx'=16,'gy'=4,'gz'=8] {'gx','gy','gz'}, use_global_device_ids=true, to_apply=%region_30.31 | all-reduce | flops 2 | bytes 16 | tf_op jit(solution)/shard_map/psum | solution.py:140
  1045.4 8.4 collective-permute-done.91
  1086.6 103.1 %psum.92 = f32[]{:T(128)} all-reduce(f32[]{:T(128)} %get-tuple-element.24), channel_id=1, replica_groups=mesh['gx'=16,'gy'=4,'gz'=8] {'gx','gy','gz'}, use_global_device_ids=true, to_apply=%region_35.36 | all-reduce | flops 1 | bytes 8 | tf_op jit(solution)/shard_map/psum | solution.py:140
  1198.2 8.4 collective-permute-done.97
  1219.8 103.1 %psum.93 = f32[]{:T(128)} all-reduce(f32[]{:T(128)} %get-tuple-element.22), channel_id=1, replica_groups=mesh['gx'=16,'gy'=4,'gz'=8] {'gx','gy','gz'}, use_global_device_ids=true, to_apply=%region_37.38 | all-reduce | flops 1 | bytes 8 | tf_op jit(solution)/shard_map/psum | solution.py:163
  1334.8 8.4 collective-permute-done.109
  1375.9 103.1 %psum.94 = f32[]{:T(128)} all-reduce(f32[]{:T(128)} %get-tuple-element.18), channel_id=1, replica_groups=mesh['gx'=16,'gy'=4,'gz'=8] {'gx','gy','gz'}, use_global_device_ids=true, to_apply=%region_40.41 | all-reduce | flops 1 | bytes 8 | tf_op jit(solution)/shard_map/psum | solution.py:140
  1487.5 8.4 collective-permute-done.115
  1509.2 102.8 %psum.95 = f32[]{:T(128)} all-reduce(f32[]{:T(128)} %fusion.34), channel_id=1, replica_groups=mesh['gx'=16,'gy'=4,'gz'=8] {'gx','gy','gz'}, use_global_device_ids=true, to_apply=%region_42.43 | all-reduce | flops 1 | bytes 8 | tf_op jit(solution)/shard_map/psum | solution.py:163
  1622.8 8.5 collective-permute-done.120
  (527 shorter events, 473.1 us)
Async XLA Ops:
  1.4 17.7 %collective-permute-start.1 = (f32[2,1,8,128]{3,2,1,0:T(8,128)S(1)}, f32[2,1,8,128]{3,2,1,0:T(8,128)S(1)}, u32[]{:S(2)}, u32[]{:S(2)}) collective-permute-start(f32[2,1,8,128]{3,2,1,0:T(8,128)S(1)} %get-tuple-element.147), channel_id=1, source_target_pairs={{32,0},{64,32},{96,64},{128,96},{160,128},{192,160},{224,192},{256... | collective-permute-start | bytes 24584 | tf_op jit(solution)/shard_map/ppermute | solution.py:22
  17.1 10.4 collective-permute-start
  53.6 10.3 collective-permute-start.13
  64.0 13.0 collective-permute-start.14
  73.5 10.4 collective-permute-start.7
  103.3 10.4 collective-permute-start.19
  251.2 11.1 collective-permute-start.32
  258.9 10.4 collective-permute-start.25
  395.9 10.4 collective-permute-start.37
  540.7 10.8 collective-permute-start.50
  548.1 10.4 collective-permute-start.43
  685.1 10.4 collective-permute-start.55
  818.3 10.4 collective-permute-start.60
  862.8 13.0 collective-permute-start.74
  870.5 11.0 collective-permute-start.66
  872.4 10.4 collective-permute-start.67
  903.8 10.4 collective-permute-start.79
  1053.8 10.6 collective-permute-start.92
  1061.1 10.4 collective-permute-start.85
  1196.3 10.4 collective-permute-start.97
  1343.2 10.6 collective-permute-start.110
  1350.5 10.4 collective-permute-start.103
  1485.6 10.4 collective-permute-start.115
  1620.8 10.4 collective-permute-start.120
  (107 other events, 726.4 us)
where the time goes:
time: 1650 us
  blocking collectives  1030 us (62%)
  starting transfers between devices  388 us (24%)
  waiting for transfers between devices  170 us (10%)
  local copies, waits for them, and re-layouts  24 us (1%)
  between operations  16.5 us (1%)
    psum x6, blocking collectives, precond_sum(): return lax.psum(jnp.sum(remain * zed), ('gx', 'gy', 'gz'))  618 us
    psum x4, blocking collectives, local(): alpha = rz_now / lax.psum(jnp.sum(search * image), ('gx', 'gy', 'gz'))  412 us
    ppermute x63, starting transfers between devices, padded_2(): lax.ppermute(lax.slice_in_dim(block, 0, width, axis=dim), axis, backward)  272 us
    ppermute x63, waiting for transfers between devices, padded_2(): lax.ppermute(lax.slice_in_dim(block, block.shape[dim] - width, None, axis...  148 us
    ppermute x63, starting transfers between devices, padded_2(): lax.ppermute(lax.slice_in_dim(block, block.shape[dim] - width, None, axis...  116 us
  transfers between devices with their start and end apart: 126, of which 64 were waited for; matrix products, arithmetic and copies ran while one was open for 0% of the time, Pallas kernels for 0%

commit v1 on v0

v1 whole, which is shorter than its diff:
```python
import functools

import jax
import jax.numpy as jnp
from jax import lax
from jax.experimental import pallas as pl
from jax.experimental.pallas import tpu as pltpu
from jax.sharding import PartitionSpec as P

NEWTON = 2
KRYLOV = 3
EPS_SQUARE = 0.25
SCALE, SHIFT = 0.7, 1.0
MESH = pl.DeviceIdType.MESH

LINE = 128
ROWS = 8


def chebyshev_pair(low):
    centre = (2.0 + low) / 2.0
    half_width = (2.0 - low) / 2.0
    sigma = centre / half_width
    rho = 1.0 / sigma
    rho_new = 1.0 / (2.0 * sigma - rho)
    last = 2.0 * rho_new / half_width
    return (1.0 + rho_new * rho) / centre + last * (1.0 - 1.0 / centre), last / centre


FINE_OWN, FINE_NEAR = chebyshev_pair(0.3)
COARSE_OWN, COARSE_NEAR = chebyshev_pair(0.05)

CROSS = [(0, 0), (1, 0), (-1, 0), (0, 1), (0, -1)]
CORNERS = [(1, 1), (1, -1), (-1, 1), (-1, -1)]


def up(field, axis):
    return pltpu.roll(field, field.shape[axis] - 1, axis)


def down(field, axis):
    return pltpu.roll(field, 1, axis)


def index_of(shape, axis):
    return lax.broadcasted_iota(jnp.int32, shape, axis)


def face_terms(mean_k, difference):
    square = difference * difference
    inverse_root = lax.rsqrt(EPS_SQUARE + square)
    root = (EPS_SQUARE + square) * inverse_root
    return mean_k * root * difference, mean_k * (EPS_SQUARE + 2.0 * square) * inverse_root


def mean_of(one, other):
    return 2.0 * one * other / (one + other)


def fold_rows(field):
    row = index_of((ROWS, field.shape[1]), 0)
    return jnp.concatenate([field[8:16], jnp.where(row < 4, field[16:24], field[0:8])], axis=0)


def pair_sum(field, axis):
    odd = lax.rem(index_of(field.shape, axis), 2) == 1
    return field + jnp.where(odd, down(field, axis), up(field, axis))


def plane_sum(field):
    return pair_sum(pair_sum(field, 0), 1)


def kernel(
    sizes, u_ref, k_ref, r_ref, s_ref, out_u, out_f,
    raw0, zed0, raw_h, zed_h, raw_e, zed_e, pack, box_u, mean_x, mean_y, mean_z, react, src,
    v0, inv, wx, wyu, wyl, wzu, wzl, cinv, cwx, cwyu, cwyl, cwzu, cwzl, zs, sums, got1, got2, got3, dummy,
    send_sem, recv_sem,
):
    nx, ny, nz = sizes
    mx, my, mz = lax.axis_index("gx"), lax.axis_index("gy"), lax.axis_index("gz")

    def block_at(dx, dy, dz):
        return (lax.rem(mx + dx + nx, nx), lax.rem(my + dy + ny, ny), lax.rem(mz + dz + nz, nz))

    core_line = [(mx, my, (mz // 2) * 2 + 1 - lax.rem(mz, 2))]
    plane = 4 * (nz // 2)
    here = lax.rem(mx, 4) * (nz // 2) + mz // 2
    plane_line = []
    for step in range(1, plane):
        there = lax.rem(here + step, plane)
        plane_line.append(
            ((mx // 4) * 4 + there // (nz // 2), my, lax.rem(there, nz // 2) * 2 + lax.rem(mz, 2))
        )
    line = (nx // 4) * ny
    at = (mx // 4) * ny + my
    long_line = []
    for step in range(1, line):
        there = lax.rem(at + step, line)
        long_line.append(((there // ny) * 4 + lax.rem(mx, 4), lax.rem(there, ny), mz))

    offsets = [(dx, dy, dz) for dx in (-1, 0, 1) for dy in (-1, 0, 1) for dz in (-1, 0, 1)]
    offsets = [d for d in offsets if d != (0, 0, 0)] + [(2, 0, 0), (-2, 0, 0)]

    zero24 = jnp.zeros((24, LINE), jnp.float32)
    for e in range(4):
        for i in range(12):
            raw_e[e, i] = zero24
    for f in range(4):
        for i in range(14):
            raw0[f, i] = zero24
    for f in range(3):
        for i in range(14):
            raw_h[f, i] = zero24
    for ref, f in ((u_ref, 0), (k_ref, 1), (r_ref, 2), (s_ref, 3)):
        raw0[f, 5:9, 8:16] = ref[...]

    barrier = pltpu.get_barrier_semaphore()
    partners = [block_at(*d) for d in offsets] + core_line + plane_line + long_line
    for partner in partners:
        pl.semaphore_signal(barrier, inc=1, device_id=partner, device_id_type=MESH)

    lane = index_of((ROWS, LINE), 1)
    copies = []

    def send(source, target, slot, device):
        copy = pltpu.make_async_remote_copy(
            source, target, send_sem.at[0], recv_sem.at[slot], device_id=device, device_id_type=MESH
        )
        copy.start()
        copies.append(copy)

    def receive(tiles, slot):
        part = dummy.at[pl.ds(0, tiles)]
        pltpu.make_async_copy(part, part, recv_sem.at[slot]).wait()

    def pack_z(tiles, place):
        low = jnp.zeros((ROWS, LINE), jnp.float32)
        high = low
        for g, tile in enumerate(tiles):
            mine = lane // 8 == g
            low = jnp.where(mine, tile if g == 0 else pltpu.roll(tile, 8 * g, 1), low)
            shift = (8 * g + 8) % LINE
            high = jnp.where(mine, pltpu.roll(tile, shift, 1) if shift else tile, high)
        pack[place, 0] = low
        pack[place, 1] = high

    def unpack_z(low_tile, high_tile, g):
        shift = (LINE - 8 * g) % LINE
        above = pltpu.roll(low_tile, shift, 1) if shift else low_tile
        shift = (LINE - 8 - 8 * g) % LINE
        below = pltpu.roll(high_tile, shift, 1) if shift else high_tile
        return jnp.where(lane < 64, above, below)

    def exchange_wide(raw, zed, place, fields, far, slot):
        everything = pl.ds(0, fields)
        own = (everything, pl.ds(5, 4), pl.ds(8, 8))
        for dx, dy in CORNERS:
            target = (everything, pl.ds(5 - 4 * dx, 4), pl.ds(8 - 8 * dy, 8))
            send(raw.at[own], raw.at[target], slot, block_at(dx, dy, 0))
        for dx, dy in CORNERS + CROSS:
            for dz in (1, -1):
                send(
                    pack.at[place, (1 + dz) // 2],
                    zed.at[1 - dx, 1 - dy, (1 - dz) // 2],
                    slot,
                    block_at(dx, dy, dz),
                )
        some = pl.ds(0, far)
        rows = pl.ds(8, 8)
        send(raw.at[some, pl.ds(8, 1), rows], raw.at[some, pl.ds(0, 1), rows], slot, block_at(2, 0, 0))
        send(raw.at[some, pl.ds(5, 1), rows], raw.at[some, pl.ds(13, 1), rows], slot, block_at(-2, 0, 0))
        for dx, dy in CROSS[1:]:
            target = (everything, pl.ds(5 - 4 * dx, 4), pl.ds(8 - 8 * dy, 8))
            send(raw.at[own], raw.at[target], slot, block_at(dx, dy, 0))
        return 16 * fields + 18 + 2 * far + 16 * fields

    def wide_slab(raw, zed, field, i):
        main = raw[field, i]
        if i in (0, 13):
            return jnp.concatenate([main, jnp.zeros_like(main)], axis=1)
        column, s = divmod(i - 1, 4)
        g = field * 4 + s
        halo = [unpack_z(zed[column, y, 1], zed[column, y, 0], g) for y in range(3)]
        return jnp.concatenate([main, jnp.concatenate(halo, axis=0)], axis=1)

    def exchange_v(tiles, e):
        place, slot = 2 + e, 2 + e
        for s in range(4):
            raw_e[e, 4 + s, 8:16] = tiles[s]
        pack_z(tiles, place)
        raw, zed = raw_e.at[e], zed_e.at[e]
        rows = pl.ds(8, 8)
        for dx, dy in CORNERS:
            source = (pl.ds(6 if dx > 0 else 4, 2), rows)
            target = (pl.ds(2 if dx > 0 else 8, 2), pl.ds(8 - 8 * dy, 8))
            send(raw.at[source], raw.at[target], slot, block_at(dx, dy, 0))
        for dx, dy in CROSS:
            for dz in (1, -1):
                send(
                    pack.at[place, (1 + dz) // 2],
                    zed.at[1 - dx, 1 - dy, (1 - dz) // 2],
                    slot,
                    block_at(dx, dy, dz),
                )
        for dx, dy in CROSS[1:]:
            target = (pl.ds(4 - 4 * dx, 4), pl.ds(8 - 8 * dy, 8))
            send(raw.at[pl.ds(4, 4), rows], raw.at[target], slot, block_at(dx, dy, 0))
        receive(8 + 10 + 16, slot)
        slabs = []
        nothing = jnp.zeros((ROWS, LINE), jnp.float32)
        row = index_of((ROWS, LINE), 0)
        for i in range(12):
            main = fold_rows(raw_e[e, i])
            column, s = divmod(i, 4)
            own_halo, side_halo = nothing, nothing
            if 2 <= i < 10:
                own_halo = unpack_z(zed_e[e, column, 1, 1], zed_e[e, column, 1, 0], s)
            if 4 <= i < 8:
                side_halo = jnp.where(
                    row < 4,
                    unpack_z(zed_e[e, 1, 2, 1], zed_e[e, 1, 2, 0], s),
                    unpack_z(zed_e[e, 1, 0, 1], zed_e[e, 1, 0, 0], s),
                )
            slabs.append(jnp.concatenate([main, jnp.concatenate([own_halo, side_halo], axis=0)], axis=1))
        return slabs

    def coefficients():
        face_x = [face_terms(mean_x[i], box_u[i + 1] - box_u[i]) for i in range(13)]
        cface = []
        for j in range(7):
            cface.append(plane_sum(face_x[2 * j][1]))
            if 1 <= j < 6:
                cwx[j - 1] = fold_rows(cface[j])
        for i in range(7):
            wx[i] = fold_rows(face_x[i + 3][1])
        for c in range(6):
            pair_y, pair_z, pair_r = None, None, None
            for half in range(2):
                i = 2 * c + half
                u = box_u[i + 1]
                re = react[i]
                flux_y, w_y = face_terms(mean_y[i], up(u, 0) - u)
                flux_z, w_z = face_terms(mean_z[i], up(u, 1) - u)
                low_y, low_z = down(w_y, 0), down(w_z, 1)
                force = (
                    src[i]
                    - re * u
                    + (face_x[i + 1][0] - face_x[i][0])
                    + (flux_y - down(flux_y, 0))
                    + (flux_z - down(flux_z, 1))
                )
                v0[i] = fold_rows(force)
                if 2 <= i < 10:
                    diagonal = re + face_x[i + 1][1] + face_x[i][1] + w_y + low_y + w_z + low_z
                    inv[i - 2] = fold_rows(1.0 / diagonal)
                if 3 <= i < 9:
                    wyu[i - 3] = fold_rows(w_y)
                    wyl[i - 3] = fold_rows(low_y)
                    wzu[i - 3] = fold_rows(w_z)
                    wzl[i - 3] = fold_rows(low_z)
                pair_y = w_y if half == 0 else pair_y + w_y
                pair_z = w_z if half == 0 else pair_z + w_z
                pair_r = re if half == 0 else pair_r + re
            odd_row = lax.rem(index_of((24, 2 * LINE), 0), 2) == 1
            odd_lane = lax.rem(index_of((24, 2 * LINE), 1), 2) == 1
            sum_y = pair_sum(jnp.where(odd_row, pair_y, up(pair_y, 0)), 1)
            sum_z = pair_sum(jnp.where(odd_lane, pair_z, up(pair_z, 1)), 0)
            low_y, low_z = pltpu.roll(sum_y, 2, 0), pltpu.roll(sum_z, 2, 1)
            diagonal = plane_sum(pair_r) + cface[c] + cface[c + 1] + sum_y + low_y + sum_z + low_z
            cinv[c] = fold_rows(1.0 / diagonal)
            if 1 <= c < 5:
                cwyu[c - 1] = fold_rows(sum_y)
                cwyl[c - 1] = fold_rows(low_y)
                cwzu[c - 1] = fold_rows(sum_z)
                cwzl[c - 1] = fold_rows(low_z)

    def precondition(v, j):
        own = [inv[i] * v[i + 2] for i in range(8)]
        coarse = [cinv[c] * plane_sum(v[2 * c] + v[2 * c + 1]) for c in range(6)]
        coarse_z = []
        for c in range(4):
            q = coarse[c + 1]
            near = (
                cwx[c] * coarse[c]
                + cwx[c + 1] * coarse[c + 2]
                + cwyu[c] * pltpu.roll(q, 14, 0)
                + cwyl[c] * pltpu.roll(q, 2, 0)
                + cwzu[c] * pltpu.roll(q, 2 * LINE - 2, 1)
                + cwzl[c] * pltpu.roll(q, 2, 1)
            )
            coarse_z.append(COARSE_OWN * q + COARSE_NEAR * (cinv[c + 1] * near))
        for i in range(6):
            q = own[i + 1]
            near = (
                wx[i] * own[i]
                + wx[i + 1] * own[i + 2]
                + wyu[i] * up(q, 0)
                + wyl[i] * down(q, 0)
                + wzu[i] * up(q, 1)
                + wzl[i] * down(q, 1)
            )
            zs[j, i] = FINE_OWN * q + FINE_NEAR * (inv[i + 1] * near) + coarse_z[(i + 1) // 2]

    def image(j, s):
        i = s + 1
        mid = zs[j, i]
        here = mid[0:8, 0:LINE]
        tall, wide = mid[:, 0:LINE], mid[0:8, :]
        own = (slice(0, 8), slice(0, LINE))
        total = react[i + 3, 8:16, 0:LINE] * here
        for weight, other in (
            (wx[(i,) + own], zs[(j, i - 1) + own]),
            (wx[(i + 1,) + own], zs[(j, i + 1) + own]),
            (wyu[(i,) + own], up(tall, 0)[0:8]),
            (wyl[(i,) + own], down(tall, 0)[0:8]),
            (wzu[(i,) + own], up(wide, 1)[:, 0:LINE]),
            (wzl[(i,) + own], down(wide, 1)[:, 0:LINE]),
        ):
            total = total + weight * (here - other)
        return total

    def global_sum(rows, which, between):
        group = index_of((1, LINE), 1) // 16
        mixed = jnp.zeros((1, LINE), jnp.float32)
        for n, row in enumerate(rows):
            row = jnp.sum(row, axis=0, keepdims=True)
            for shift in (64, 32, 16):
                row = row + pltpu.roll(row, shift, 1)
            mixed = jnp.where(group == n, row, mixed)
        phases = ((core_line, got1), (plane_line, got2), (long_line, got3))
        for phase, (partners, got) in enumerate(phases):
            sums[which, phase] = mixed
            slot = 6 + 3 * which + phase
            for n, partner in enumerate(partners):
                send(sums.at[which, phase], got.at[which, n], slot, partner)
            if phase == 0:
                between()
            part = got.at[which]
            pltpu.make_async_copy(part, part, recv_sem.at[slot]).wait()
            mixed = mixed + jnp.sum(got[which], axis=0)
        return [jnp.sum(jnp.where(group == n, mixed, 0.0), axis=1, keepdims=True) for n in range(6)]

    def solve(m):
        h = [(m[n + 1] + SHIFT * m[n]) * (1.0 / SCALE) for n in range(5)]

        def inverse(pivot, of):
            good = pivot > 1e-6 * of
            return jnp.where(good, 1.0 / jnp.where(good, pivot, 1.0), 0.0)

        i0 = inverse(h[0], jnp.zeros_like(h[0]))
        l1, l2 = h[1] * i0, h[2] * i0
        i1 = inverse(h[2] - l1 * h[1], h[2])
        h21 = h[3] - l2 * h[1]
        l21 = h21 * i1
        i2 = inverse(h[4] - l2 * h[2] - l21 * h21, h[4])
        y0 = m[0]
        y1 = m[1] - l1 * y0
        y2 = m[2] - l2 * y0 - l21 * y1
        c2 = y2 * i2
        c1 = y1 * i1 - l21 * c2
        c0 = y0 * i0 - l1 * c1 - l2 * c2
        return c0, c1, c2

    def total_of(tiles, others):
        total = tiles[0] * others[0]
        for s in range(1, 4):
            total = total + tiles[s] * others[s]
        return total

    pack_z([raw0[f, 5 + s, 8:16] for f in range(4) for s in range(4)], 0)
    pl.semaphore_wait(barrier, len(partners))
    count = exchange_wide(raw0, zed0, 0, 4, 2, 0)
    receive(count, 0)
    for i in range(14):
        box_u[i] = wide_slab(raw0, zed0, 0, i)
    k_slabs = [wide_slab(raw0, zed0, 1, i) for i in range(14)]
    for i in range(13):
        mean_x[i] = mean_of(k_slabs[i], k_slabs[i + 1])
    for i in range(12):
        k = k_slabs[i + 1]
        mean_y[i] = mean_of(k, up(k, 0))
        mean_z[i] = mean_of(k, up(k, 1))
        react[i] = wide_slab(raw0, zed0, 2, i + 1)
        src[i] = wide_slab(raw0, zed0, 3, i + 1)

    own = (slice(0, 8), slice(0, LINE))
    for newton in range(NEWTON):
        coefficients()
        rows = []
        v = [v0[i] for i in range(12)]
        tiles = [slab[0:8, 0:LINE] for slab in v[4:8]]
        for j in range(KRYLOV):
            precondition(v, j)
            z_tiles = [zs[(j, s + 1) + own] for s in range(4)]
            rows.append(total_of(tiles, z_tiles))
            if newton + 1 < NEWTON:
                for s in range(4):
                    raw_h[j, 5 + s, 8:16] = z_tiles[s]
            tiles = [SCALE * image(j, s) - SHIFT * tiles[s] for s in range(4)]
            rows.append(total_of(tiles, z_tiles))
            if j + 1 < KRYLOV:
                v = exchange_v(tiles, 2 * newton + j)

        def beside(newton=newton):
            if newton + 1 < NEWTON:
                pack_z([raw_h[f, 5 + s, 8:16] for f in range(3) for s in range(4)], 1)
                exchange_wide(raw_h, zed_h, 1, 3, 3, 1)

        c = solve(global_sum(rows, newton, beside))
        if newton + 1 < NEWTON:
            receive(32 * 3 + 18 + 6, 1)
            for i in range(14):
                total = box_u[i]
                for j in range(3):
                    total = total + c[j] * wide_slab(raw_h, zed_h, j, i)
                box_u[i] = total

    last = []
    for i in range(6):
        total = fold_rows(box_u[i + 4])
        for j in range(3):
            total = total + c[j] * zs[j, i]
        last.append(total)
    low_flux = None
    for s in range(-1, 4):
        lower, upper = last[s + 1][own], last[s + 2][own]
        flux, _ = face_terms(mean_x[s + 5, 8:16, 0:LINE], upper - lower)
        if s >= 0:
            mid = last[s + 1]
            tall = mid[:, 0:LINE]
            wide = mid[0:8, :]
            out_u[s] = lower
            flux_y, _ = face_terms(fold_rows(mean_y[s + 4, :, 0:LINE]), up(tall, 0) - tall)
            flux_z, _ = face_terms(mean_z[s + 4, 8:16, :], up(wide, 1) - wide)
            out_f[s] = (
                react[s + 4, 8:16, 0:LINE] * lower
                - (flux - low_flux)
                - (flux_y - down(flux_y, 0))[0:8]
                - (flux_z - down(flux_z, 1))[:, 0:LINE]
                - src[s + 4, 8:16, 0:LINE]
            )
        low_flux = flux
    for copy in copies:
        copy.wait_send()


def local(sizes, state, conductivity, reaction, source):
    nx, ny, nz = sizes
    plane, line = 4 * (nz // 2), (nx // 4) * ny

    def vmem(*shape):
        return pltpu.VMEM(shape, jnp.float32)

    full, half = (24, 2 * LINE), (16, 2 * LINE)
    tile = (ROWS, LINE)
    scratch = [
        vmem(4, 14, 24, LINE), vmem(3, 3, 2, *tile), vmem(3, 14, 24, LINE), vmem(3, 3, 2, *tile),
        vmem(4, 12, 24, LINE), vmem(4, 3, 3, 2, *tile), vmem(6, 2, *tile), vmem(14, *full),
        vmem(13, *full), vmem(12, *full), vmem(12, *full), vmem(12, *full), vmem(12, *full),
        vmem(12, *half), vmem(8, *half), vmem(7, *half), vmem(6, *half), vmem(6, *half), vmem(6, *half), vmem(6, *half),
        vmem(6, *half), vmem(5, *half), vmem(4, *half), vmem(4, *half), vmem(4, *half), vmem(4, *half),
        vmem(3, 6, *half), vmem(2, 3, 1, LINE), vmem(2, 1, 1, LINE), vmem(2, plane - 1, 1, LINE), vmem(2, line - 1, 1, LINE),
        vmem(160, *tile), pltpu.SemaphoreType.DMA((1,)), pltpu.SemaphoreType.DMA((12,)),
    ]
    spec = pl.BlockSpec(memory_space=pltpu.VMEM)
    return pl.pallas_call(
        functools.partial(kernel, sizes),
        out_shape=[jax.ShapeDtypeStruct(state.shape, jnp.float32)] * 2,
        in_specs=[spec] * 4,
        out_specs=[spec] * 2,
        scratch_shapes=scratch,
        compiler_params=pltpu.CompilerParams(
            collective_id=0, has_side_effects=True, vmem_limit_bytes=32 * 1024 * 1024
        ),
    )(state, conductivity, reaction, source)


def solution(mesh):
    sizes = tuple(mesh.shape[name] for name in ("gx", "gy", "gz"))
    placed = P("gx", "gy", "gz")
    return jax.shard_map(
        functools.partial(local, sizes),
        mesh=mesh,
        in_specs=(placed,) * 4,
        out_specs=(placed, placed),
        check_vma=False,
    )
```

time: 1650 us -> 125 us (0.08)
  blocking collectives: 1030 us -> 0 us
  starting transfers between devices: 388 us -> 0 us
  waiting for transfers between devices: 170 us -> 0 us
  Pallas kernels: 0 us -> 120 us
  local copies, waits for them, and re-layouts: 24 us -> 4.07 us
    psum x10 -> x0, blocking collectives: 1030 us -> none  [the longest x6 618 us: precond_sum(): return lax.psum(jnp.sum(remain * zed), ('gx', 'gy', 'gz'))]
    ppermute x126 -> x0, starting transfers between devices: 388 us -> none  [the longest x63 272 us: padded_2(): lax.ppermute(lax.slice_in_dim(block, 0, width, axis=dim), axis, backward)]
    ppermute x126 -> x0, waiting for transfers between devices: 170 us -> none  [the longest x63 148 us: padded_2(): lax.ppermute(lax.slice_in_dim(block, block.shape[dim] - width, None, axis...]
    pallas_call x0 -> x1, Pallas kernels: none -> 120 us  [local(): pl.pallas_call(functools.partial(kernel, sizes), out_shape=[jax.ShapeDtyp...]
    reshape x31 -> x0, local copies, waits for them, and re-layouts: 20.2 us -> none  [the longest x19 19.1 us: restrict(): field.reshape(first // 2, 2, second // 2, 2, third // 2, 2)]
  transfers between devices with their start and end apart: 126 -> 0, of which waited for: 64 -> 0; matrix products, arithmetic and copies ran while one was open for 0% -> 0% of each run, Pallas kernels for 0% -> 0%
where the time goes in v1:
time: 125 us
  Pallas kernels  120 us (96%)
  local copies, waits for them, and re-layouts  4.07 us (3%)
    pallas_call x1, Pallas kernels, local(): pl.pallas_call(functools.partial(kernel, sizes), out_shape=[jax.ShapeDtyp...  120 us
    unnamed x10, local copies, waits for them, and re-layouts  4.07 us

profile of v1, /device:TPU:1, one launch (start us, length us, event | category | flops | bytes accessed | tf_op | source)
XLA Modules:
  0.0 124.8 jit_solution(104402749968709099)
XLA Ops:
  0.6 0.0 copy-start
  0.6 0.7 copy-done
  1.3 0.0 copy-start.1
  1.4 0.7 copy-done.1
  2.1 0.0 copy-start.2
  2.1 0.7 copy-done.2
  2.8 0.0 copy-start.3
  2.8 0.7 copy-done.3
  3.5 120.1 %shard_map.59 = (f32[4,8,128]{2,1,0:T(8,128)S(1)}, f32[4,8,128]{2,1,0:T(8,128)S(1)}) custom-call(f32[4,8,128]{2,1,0:T(8,128)S(1)} %copy-done, f32[4,8,128]{2,1,0:T(8,128)S(1)} %copy-done.1, f32[4,8,128]{2,1,0:T(8,128)S(1)} %copy-done.2, f32[4,8,128]{2,1,0:T(8,128)S(1)} %copy-done.3), custom_call_target="tpu_custom_call" | custom-call | tf_op jit(solution)/shard_map/pallas_call | solution.py:467
  123.6 0.6 copy.8
  124.2 0.6 copy.9
Async XLA Ops:
  0.6 0.7 copy-start
  1.3 0.7 copy-start.1
  2.1 0.7 copy-start.2
  2.8 0.7 copy-start.3

commit v2 on v1

--- a/solution.py
+++ b/solution.py
@@ -74,14 +74,20 @@
 def kernel(
     sizes, u_ref, k_ref, r_ref, s_ref, out_u, out_f,
     raw0, zed0, raw_h, zed_h, raw_e, zed_e, pack, box_u, mean_x, mean_y, mean_z, react, src,
-    v0, inv, wx, wyu, wyl, wzu, wzl, cinv, cwx, cwyu, cwyl, cwzu, cwzl, zs, sums, got1, got2, got3, dummy,
+    v0, inv, wx, wyu, wyl, wzu, wzl, cinv, cwx, cwyu, cwyl, cwzu, cwzl, zs, sums, got1, got2, got3, ends, dummy,
     send_sem, recv_sem,
 ):
     nx, ny, nz = sizes
     mx, my, mz = lax.axis_index("gx"), lax.axis_index("gy"), lax.axis_index("gz")
 
+    group, place_y = mx // 4, lax.rem(mx, 4)
+    bx, by = group * 4 + my, place_y
+    partner = (group * 4 + my, place_y, mz)
+    alone = my == place_y
+
     def block_at(dx, dy, dz):
-        return (lax.rem(mx + dx + nx, nx), lax.rem(my + dy + ny, ny), lax.rem(mz + dz + nz, nz))
+        x, y = lax.rem(bx + dx + nx, nx), lax.rem(by + dy + ny, ny)
+        return ((x // 4) * 4 + y, lax.rem(x, 4), lax.rem(mz + dz + nz, nz))
 
     core_line = [(mx, my, (mz // 2) * 2 + 1 - lax.rem(mz, 2))]
     plane = 4 * (nz // 2)
@@ -102,23 +108,15 @@
     offsets = [(dx, dy, dz) for dx in (-1, 0, 1) for dy in (-1, 0, 1) for dz in (-1, 0, 1)]
     offsets = [d for d in offsets if d != (0, 0, 0)] + [(2, 0, 0), (-2, 0, 0)]
 
-    zero24 = jnp.zeros((24, LINE), jnp.float32)
-    for e in range(4):
-        for i in range(12):
-            raw_e[e, i] = zero24
-    for f in range(4):
-        for i in range(14):
-            raw0[f, i] = zero24
-    for f in range(3):
-        for i in range(14):
-            raw_h[f, i] = zero24
-    for ref, f in ((u_ref, 0), (k_ref, 1), (r_ref, 2), (s_ref, 3)):
-        raw0[f, 5:9, 8:16] = ref[...]
-
     barrier = pltpu.get_barrier_semaphore()
     partners = [block_at(*d) for d in offsets] + core_line + plane_line + long_line
-    for partner in partners:
+
+    @pl.when(jnp.logical_not(alone))
+    def _():
         pl.semaphore_signal(barrier, inc=1, device_id=partner, device_id_type=MESH)
+
+    for other in partners:
+        pl.semaphore_signal(barrier, inc=1, device_id=other, device_id_type=MESH)
 
     lane = index_of((ROWS, LINE), 1)
     copies = []
@@ -176,9 +174,11 @@
         return 16 * fields + 18 + 2 * far + 16 * fields
 
     def wide_slab(raw, zed, field, i):
+        if i in (0, 13):
+            nothing = jnp.zeros((ROWS, LINE), jnp.float32)
+            main = jnp.concatenate([nothing, raw[field, i, 8:16], nothing], axis=0)
+            return jnp.concatenate([main, jnp.zeros_like(main)], axis=1)
         main = raw[field, i]
-        if i in (0, 13):
-            return jnp.concatenate([main, jnp.zeros_like(main)], axis=1)
         column, s = divmod(i - 1, 4)
         g = field * 4 + s
         halo = [unpack_z(zed[column, y, 1], zed[column, y, 0], g) for y in range(3)]
@@ -211,7 +211,10 @@
         nothing = jnp.zeros((ROWS, LINE), jnp.float32)
         row = index_of((ROWS, LINE), 0)
         for i in range(12):
-            main = fold_rows(raw_e[e, i])
+            if 2 <= i < 10:
+                main = fold_rows(raw_e[e, i])
+            else:
+                main = jnp.concatenate([raw_e[e, i, 8:16], nothing], axis=0)
             column, s = divmod(i, 4)
             own_halo, side_halo = nothing, nothing
             if 2 <= i < 10:
@@ -368,8 +371,29 @@
             total = total + tiles[s] * others[s]
         return total
 
+    def swap(sources, targets, slot):
+        @pl.when(alone)
+        def _():
+            for source, target in zip(sources, targets):
+                pltpu.make_async_copy(source, target, recv_sem.at[slot]).start()
+
+        @pl.when(jnp.logical_not(alone))
+        def _():
+            for source, target in zip(sources, targets):
+                pltpu.make_async_remote_copy(
+                    source, target, send_sem.at[0], recv_sem.at[slot], device_id=partner, device_id_type=MESH
+                ).start()
+
+        receive(4 * len(sources), slot)
+
+        @pl.when(jnp.logical_not(alone))
+        def _():
+            part = dummy.at[pl.ds(0, 4 * len(sources))]
+            pltpu.make_async_copy(part, part, send_sem.at[0]).wait()
+
+    pl.semaphore_wait(barrier, len(partners) + 1 - alone.astype(jnp.int32))
+    swap([u_ref, k_ref, r_ref, s_ref], [raw0.at[f, pl.ds(5, 4), pl.ds(8, 8)] for f in range(4)], 12)
     pack_z([raw0[f, 5 + s, 8:16] for f in range(4) for s in range(4)], 0)
-    pl.semaphore_wait(barrier, len(partners))
     count = exchange_wide(raw0, zed0, 0, 4, 2, 0)
     receive(count, 0)
     for i in range(14):
@@ -430,10 +454,10 @@
             mid = last[s + 1]
             tall = mid[:, 0:LINE]
             wide = mid[0:8, :]
-            out_u[s] = lower
+            ends[0, s] = lower
             flux_y, _ = face_terms(fold_rows(mean_y[s + 4, :, 0:LINE]), up(tall, 0) - tall)
             flux_z, _ = face_terms(mean_z[s + 4, 8:16, :], up(wide, 1) - wide)
-            out_f[s] = (
+            ends[1, s] = (
                 react[s + 4, 8:16, 0:LINE] * lower
                 - (flux - low_flux)
                 - (flux_y - down(flux_y, 0))[0:8]
@@ -443,6 +467,7 @@
         low_flux = flux
     for copy in copies:
         copy.wait_send()
+    swap([ends.at[0], ends.at[1]], [out_u, out_f], 13)
 
 
 def local(sizes, state, conductivity, reaction, source):
@@ -461,9 +486,9 @@
         vmem(12, *half), vmem(8, *half), vmem(7, *half), vmem(6, *half), vmem(6, *half), vmem(6, *half), vmem(6, *half),
         vmem(6, *half), vmem(5, *half), vmem(4, *half), vmem(4, *half), vmem(4, *half), vmem(4, *half),
         vmem(3, 6, *half), vmem(2, 3, 1, LINE), vmem(2, 1, 1, LINE), vmem(2, plane - 1, 1, LINE), vmem(2, line - 1, 1, LINE),
-        vmem(160, *tile), pltpu.SemaphoreType.DMA((1,)), pltpu.SemaphoreType.DMA((12,)),
+        vmem(2, 4, *tile), vmem(160, *tile), pltpu.SemaphoreType.DMA((1,)), pltpu.SemaphoreType.DMA((14,)),
     ]
-    spec = pl.BlockSpec(memory_space=pltpu.VMEM)
+    spec = pl.BlockSpec(memory_space=pl.ANY)
     return pl.pallas_call(
         functools.partial(kernel, sizes),
         out_shape=[jax.ShapeDtypeStruct(state.shape, jnp.float32)] * 2,

time: 125 us -> 87.2 us (0.70)
  the two profiles are of different devices: /device:TPU:1 before, /device:TPU:24 now
where the time goes in v2:
time: 87.2 us; the launch traced here: 86.7 us
  Pallas kernels  82 us (94%)
  local copies, waits for them, and re-layouts  4.07 us (5%)
    pallas_call x1, Pallas kernels, local(): pl.pallas_call(functools.partial(kernel, sizes), out_shape=[jax.ShapeDtyp...  82 us
    unnamed x10, local copies, waits for them, and re-layouts  4.07 us

profile of v2, /device:TPU:24, one launch (start us, length us, event | category | flops | bytes accessed | tf_op | source)
XLA Modules:
  0.0 86.7 jit_solution(6899528272322385687)
XLA Ops:
  0.6 0.0 copy-start
  0.6 0.7 copy-done
  1.3 0.0 copy-start.1
  1.4 0.7 copy-done.1
  2.1 0.0 copy-start.2
  2.1 0.7 copy-done.2
  2.8 0.0 copy-start.3
  2.8 0.7 copy-done.3
  3.5 82.0 %shard_map.59 = (f32[4,8,128]{2,1,0:T(8,128)S(1)}, f32[4,8,128]{2,1,0:T(8,128)S(1)}) custom-call(f32[4,8,128]{2,1,0:T(8,128)S(1)} %copy-done, f32[4,8,128]{2,1,0:T(8,128)S(1)} %copy-done.1, f32[4,8,128]{2,1,0:T(8,128)S(1)} %copy-done.2, f32[4,8,128]{2,1,0:T(8,128)S(1)} %copy-done.3), custom_call_target="tpu_custom_call" | custom-call | tf_op jit(solution)/shard_map/pallas_call | solution.py:492
  85.5 0.6 copy.8
  86.1 0.6 copy.9
Async XLA Ops:
  0.6 0.7 copy-start
  1.3 0.7 copy-start.1
  2.1 0.7 copy-start.2
  2.8 0.7 copy-start.3

commit v3 on v2

--- a/solution.py
+++ b/solution.py
@@ -75,7 +75,7 @@
     sizes, u_ref, k_ref, r_ref, s_ref, out_u, out_f,
     raw0, zed0, raw_h, zed_h, raw_e, zed_e, pack, box_u, mean_x, mean_y, mean_z, react, src,
     v0, inv, wx, wyu, wyl, wzu, wzl, cinv, cwx, cwyu, cwyl, cwzu, cwzl, zs, sums, got1, got2, got3, ends, dummy,
-    send_sem, recv_sem,
+    end_zs, end_x, end_y, end_z, end_rs, send_sem, recv_sem, far_sem,
 ):
     nx, ny, nz = sizes
     mx, my, mz = lax.axis_index("gx"), lax.axis_index("gy"), lax.axis_index("gz")
@@ -109,7 +109,8 @@
     offsets = [d for d in offsets if d != (0, 0, 0)] + [(2, 0, 0), (-2, 0, 0)]
 
     barrier = pltpu.get_barrier_semaphore()
-    partners = [block_at(*d) for d in offsets] + core_line + plane_line + long_line
+    partners = [block_at(*d) for d in offsets]
+    far_ones = [(lax.rem(mx + 4, nx), my, mz), (lax.rem(mx + nx - 4, nx), my, mz)]
 
     @pl.when(jnp.logical_not(alone))
     def _():
@@ -184,7 +185,7 @@
         halo = [unpack_z(zed[column, y, 1], zed[column, y, 0], g) for y in range(3)]
         return jnp.concatenate([main, jnp.concatenate(halo, axis=0)], axis=1)
 
-    def exchange_v(tiles, e):
+    def exchange_v(tiles, e, between):
         place, slot = 2 + e, 2 + e
         for s in range(4):
             raw_e[e, 4 + s, 8:16] = tiles[s]
@@ -206,6 +207,7 @@
         for dx, dy in CROSS[1:]:
             target = (pl.ds(4 - 4 * dx, 4), pl.ds(8 - 8 * dy, 8))
             send(raw.at[pl.ds(4, 4), rows], raw.at[target], slot, block_at(dx, dy, 0))
+        between()
         receive(8 + 10 + 16, slot)
         slabs = []
         nothing = jnp.zeros((ROWS, LINE), jnp.float32)
@@ -339,6 +341,8 @@
                 send(sums.at[which, phase], got.at[which, n], slot, partner)
             if phase == 0:
                 between()
+            if phase == 1 and which == 0:
+                pl.semaphore_wait(far_sem, 2)
             part = got.at[which]
             pltpu.make_async_copy(part, part, recv_sem.at[slot]).wait()
             mixed = mixed + jnp.sum(got[which], axis=0)
@@ -371,7 +375,9 @@
             total = total + tiles[s] * others[s]
         return total
 
-    def swap(sources, targets, slot):
+    given = []
+
+    def give(sources, targets, slot, tiles):
         @pl.when(alone)
         def _():
             for source, target in zip(sources, targets):
@@ -381,21 +387,23 @@
         def _():
             for source, target in zip(sources, targets):
                 pltpu.make_async_remote_copy(
-                    source, target, send_sem.at[0], recv_sem.at[slot], device_id=partner, device_id_type=MESH
+                    source, target, send_sem.at[1], recv_sem.at[slot], device_id=partner, device_id_type=MESH
                 ).start()
 
-        receive(4 * len(sources), slot)
-
-        @pl.when(jnp.logical_not(alone))
-        def _():
-            part = dummy.at[pl.ds(0, 4 * len(sources))]
-            pltpu.make_async_copy(part, part, send_sem.at[0]).wait()
+        given.append(tiles)
 
     pl.semaphore_wait(barrier, len(partners) + 1 - alone.astype(jnp.int32))
-    swap([u_ref, k_ref, r_ref, s_ref], [raw0.at[f, pl.ds(5, 4), pl.ds(8, 8)] for f in range(4)], 12)
+    give([u_ref, k_ref, r_ref, s_ref], [raw0.at[f, pl.ds(5, 4), pl.ds(8, 8)] for f in range(4)], 12, 16)
+    last_r = pltpu.make_async_copy(r_ref, end_rs.at[0], send_sem.at[2])
+    last_s = pltpu.make_async_copy(s_ref, end_rs.at[1], send_sem.at[3])
+    last_r.start()
+    last_s.start()
+    receive(16, 12)
     pack_z([raw0[f, 5 + s, 8:16] for f in range(4) for s in range(4)], 0)
     count = exchange_wide(raw0, zed0, 0, 4, 2, 0)
     receive(count, 0)
+    for other in far_ones:
+        pl.semaphore_signal(far_sem, inc=1, device_id=other, device_id_type=MESH)
     for i in range(14):
         box_u[i] = wide_slab(raw0, zed0, 0, i)
     k_slabs = [wide_slab(raw0, zed0, 1, i) for i in range(14)]
@@ -409,27 +417,59 @@
         src[i] = wide_slab(raw0, zed0, 3, i + 1)
 
     own = (slice(0, 8), slice(0, LINE))
+
+    def give_fields(first, count):
+        which = pl.ds(first, count)
+        middle, eight, lanes = pl.ds(1, 4), pl.ds(0, 8), pl.ds(0, LINE)
+        regions = [
+            (which, pl.ds(0, 6), eight, lanes),
+            (which, middle, pl.ds(8, 8), lanes),
+            (which, middle, eight, pl.ds(LINE, LINE)),
+        ]
+        give([zs.at[r] for r in regions], [end_zs.at[r] for r in regions], 13, 14 * count)
+
+    def beside_v(newton, j):
+        if newton == 0 and j == 0:
+            four, lanes = pl.ds(4, 4), pl.ds(0, LINE)
+            give(
+                [
+                    mean_x.at[pl.ds(4, 5), pl.ds(8, 8), lanes],
+                    mean_y.at[four, pl.ds(0, 16), lanes],
+                    mean_z.at[four, pl.ds(8, 8)],
+                ],
+                [end_x, end_y, end_z],
+                13,
+                5 + 8 + 8,
+            )
+        elif newton == 1 and j == 0:
+            give_fields(3, 1)
+        elif newton == 1:
+            give_fields(4, 2)
+
     for newton in range(NEWTON):
         coefficients()
         rows = []
         v = [v0[i] for i in range(12)]
         tiles = [slab[0:8, 0:LINE] for slab in v[4:8]]
         for j in range(KRYLOV):
-            precondition(v, j)
-            z_tiles = [zs[(j, s + 1) + own] for s in range(4)]
+            at = 4 * newton + j
+            precondition(v, at)
+            z_tiles = [zs[(at, s + 1) + own] for s in range(4)]
             rows.append(total_of(tiles, z_tiles))
             if newton + 1 < NEWTON:
                 for s in range(4):
                     raw_h[j, 5 + s, 8:16] = z_tiles[s]
-            tiles = [SCALE * image(j, s) - SHIFT * tiles[s] for s in range(4)]
+            tiles = [SCALE * image(at, s) - SHIFT * tiles[s] for s in range(4)]
             rows.append(total_of(tiles, z_tiles))
             if j + 1 < KRYLOV:
-                v = exchange_v(tiles, 2 * newton + j)
+                v = exchange_v(tiles, 2 * newton + j, functools.partial(beside_v, newton, j))
 
         def beside(newton=newton):
             if newton + 1 < NEWTON:
                 pack_z([raw_h[f, 5 + s, 8:16] for f in range(3) for s in range(4)], 1)
                 exchange_wide(raw_h, zed_h, 1, 3, 3, 1)
+            else:
+                give_fields(6, 1)
 
         c = solve(global_sum(rows, newton, beside))
         if newton + 1 < NEWTON:
@@ -439,35 +479,52 @@
                 for j in range(3):
                     total = total + c[j] * wide_slab(raw_h, zed_h, j, i)
                 box_u[i] = total
-
+                if 4 <= i < 10:
+                    zs[3, i - 4] = fold_rows(total)
+
+    last_r.wait()
+    last_s.wait()
+    receive(21 + 14 + 28 + 14, 13)
     last = []
     for i in range(6):
-        total = fold_rows(box_u[i + 4])
+        total = end_zs[3, i]
         for j in range(3):
-            total = total + c[j] * zs[j, i]
+            total = total + c[j] * end_zs[4 + j, i]
         last.append(total)
     low_flux = None
     for s in range(-1, 4):
         lower, upper = last[s + 1][own], last[s + 2][own]
-        flux, _ = face_terms(mean_x[s + 5, 8:16, 0:LINE], upper - lower)
+        flux, _ = face_terms(end_x[s + 1], upper - lower)
         if s >= 0:
             mid = last[s + 1]
             tall = mid[:, 0:LINE]
             wide = mid[0:8, :]
             ends[0, s] = lower
-            flux_y, _ = face_terms(fold_rows(mean_y[s + 4, :, 0:LINE]), up(tall, 0) - tall)
-            flux_z, _ = face_terms(mean_z[s + 4, 8:16, :], up(wide, 1) - wide)
+            near_k = jnp.concatenate([end_y[s, 8:16], end_y[s, 0:8]], axis=0)
+            flux_y, _ = face_terms(near_k, up(tall, 0) - tall)
+            flux_z, _ = face_terms(end_z[s], up(wide, 1) - wide)
             ends[1, s] = (
-                react[s + 4, 8:16, 0:LINE] * lower
+                end_rs[0, s] * lower
                 - (flux - low_flux)
                 - (flux_y - down(flux_y, 0))[0:8]
                 - (flux_z - down(flux_z, 1))[:, 0:LINE]
-                - src[s + 4, 8:16, 0:LINE]
+                - end_rs[1, s]
             )
         low_flux = flux
+    store_u = pltpu.make_async_copy(ends.at[0], out_u, send_sem.at[2])
+    store_f = pltpu.make_async_copy(ends.at[1], out_f, send_sem.at[3])
+    store_u.start()
+    store_f.start()
     for copy in copies:
         copy.wait_send()
-    swap([ends.at[0], ends.at[1]], [out_u, out_f], 13)
+
+    @pl.when(jnp.logical_not(alone))
+    def _():
+        part = dummy.at[pl.ds(0, sum(given))]
+        pltpu.make_async_copy(part, part, send_sem.at[1]).wait()
+
+    store_u.wait()
+    store_f.wait()
 
 
 def local(sizes, state, conductivity, reaction, source):
@@ -485,8 +542,10 @@
         vmem(13, *full), vmem(12, *full), vmem(12, *full), vmem(12, *full), vmem(12, *full),
         vmem(12, *half), vmem(8, *half), vmem(7, *half), vmem(6, *half), vmem(6, *half), vmem(6, *half), vmem(6, *half),
         vmem(6, *half), vmem(5, *half), vmem(4, *half), vmem(4, *half), vmem(4, *half), vmem(4, *half),
-        vmem(3, 6, *half), vmem(2, 3, 1, LINE), vmem(2, 1, 1, LINE), vmem(2, plane - 1, 1, LINE), vmem(2, line - 1, 1, LINE),
-        vmem(2, 4, *tile), vmem(160, *tile), pltpu.SemaphoreType.DMA((1,)), pltpu.SemaphoreType.DMA((14,)),
+        vmem(7, 6, *half), vmem(2, 3, 1, LINE), vmem(2, 1, 1, LINE), vmem(2, plane - 1, 1, LINE), vmem(2, line - 1, 1, LINE),
+        vmem(2, 4, *tile), vmem(160, *tile),
+        vmem(7, 6, *half), vmem(5, *tile), vmem(4, 16, LINE), vmem(4, ROWS, 2 * LINE), vmem(2, 4, *tile),
+        pltpu.SemaphoreType.DMA((4,)), pltpu.SemaphoreType.DMA((14,)), pltpu.SemaphoreType.REGULAR,
     ]
     spec = pl.BlockSpec(memory_space=pl.ANY)
     return pl.pallas_call(

time: 87.2 us -> 88.1 us (1.010)
  the two profiles are of different devices: /device:TPU:24 before, /device:TPU:1 now
where the time goes in v3:
time: 88.1 us; the launch traced here: 87.6 us
  Pallas kernels  82.9 us (94%)
  local copies, waits for them, and re-layouts  4.07 us (5%)
    pallas_call x1, Pallas kernels, local(): pl.pallas_call(functools.partial(kernel, sizes), out_shape=[jax.ShapeDtyp...  82.9 us
    unnamed x10, local copies, waits for them, and re-layouts  4.07 us

profile of v3, /device:TPU:1, one launch (start us, length us, event | category | flops | bytes accessed | tf_op | source)
XLA Modules:
  0.0 87.6 jit_solution(4150772028224239900)
XLA Ops:
  0.6 0.0 copy-start
  0.6 0.7 copy-done
  1.3 0.0 copy-start.1
  1.4 0.7 copy-done.1
  2.1 0.0 copy-start.2
  2.1 0.7 copy-done.2
  2.8 0.0 copy-start.3
  2.8 0.7 copy-done.3
  3.5 82.9 %shard_map.59 = (f32[4,8,128]{2,1,0:T(8,128)S(1)}, f32[4,8,128]{2,1,0:T(8,128)S(1)}) custom-call(f32[4,8,128]{2,1,0:T(8,128)S(1)} %copy-done, f32[4,8,128]{2,1,0:T(8,128)S(1)} %copy-done.1, f32[4,8,128]{2,1,0:T(8,128)S(1)} %copy-done.2, f32[4,8,128]{2,1,0:T(8,128)S(1)} %copy-done.3), custom_call_target="tpu_custom_call" | custom-call | tf_op jit(solution)/shard_map/pallas_call | solution.py:551
  86.4 0.6 copy.8
  87.0 0.6 copy.9
Async XLA Ops:
  0.6 0.7 copy-start
  1.3 0.7 copy-start.1
  2.1 0.7 copy-start.2
  2.8 0.7 copy-start.3

commit v4 on v3

--- a/solution.py
+++ b/solution.py
@@ -75,7 +75,7 @@
     sizes, u_ref, k_ref, r_ref, s_ref, out_u, out_f,
     raw0, zed0, raw_h, zed_h, raw_e, zed_e, pack, box_u, mean_x, mean_y, mean_z, react, src,
     v0, inv, wx, wyu, wyl, wzu, wzl, cinv, cwx, cwyu, cwyl, cwzu, cwzl, zs, sums, got1, got2, got3, ends, dummy,
-    end_zs, end_x, end_y, end_z, end_rs, send_sem, recv_sem, far_sem,
+    end_zs, end_pack, end_halo, end_x, end_y, end_z, end_rs, send_sem, recv_sem, far_sem,
 ):
     nx, ny, nz = sizes
     mx, my, mz = lax.axis_index("gx"), lax.axis_index("gy"), lax.axis_index("gz")
@@ -418,33 +418,45 @@
 
     own = (slice(0, 8), slice(0, LINE))
 
-    def give_fields(first, count):
-        which = pl.ds(first, count)
-        middle, eight, lanes = pl.ds(1, 4), pl.ds(0, 8), pl.ds(0, LINE)
-        regions = [
-            (which, pl.ds(0, 6), eight, lanes),
-            (which, middle, pl.ds(8, 8), lanes),
-            (which, middle, eight, pl.ds(LINE, LINE)),
-        ]
-        give([zs.at[r] for r in regions], [end_zs.at[r] for r in regions], 13, 14 * count)
+    def give_field(f, slot):
+        row = index_of((ROWS, LINE), 0)
+        next_rows = jnp.zeros((ROWS, LINE), jnp.float32)
+        next_lanes = next_rows
+        for s in range(4):
+            tile = pltpu.roll(zs[f, s + 1, 8:16, 0:LINE], 2 * s + 1, 0)
+            next_rows = jnp.where(row // 2 == s, tile, next_rows)
+            tile = pltpu.roll(zs[f, s + 1, 0:8, LINE : 2 * LINE], 2 * s + 1, 1)
+            next_lanes = jnp.where(lane // 2 == s, tile, next_lanes)
+        end_pack[f - 3, 0] = next_rows
+        end_pack[f - 3, 1] = next_lanes
+        region = (f, pl.ds(0, 6), pl.ds(0, 8), pl.ds(0, LINE))
+        give([zs.at[region], end_pack.at[f - 3]], [end_zs.at[f - 3], end_halo.at[f - 3]], slot, 8)
 
     def beside_v(newton, j):
         if newton == 0 and j == 0:
-            four, lanes = pl.ds(4, 4), pl.ds(0, LINE)
-            give(
-                [
-                    mean_x.at[pl.ds(4, 5), pl.ds(8, 8), lanes],
-                    mean_y.at[four, pl.ds(0, 16), lanes],
-                    mean_z.at[four, pl.ds(8, 8)],
-                ],
-                [end_x, end_y, end_z],
-                13,
-                5 + 8 + 8,
-            )
-        elif newton == 1 and j == 0:
-            give_fields(3, 1)
+            for i in range(6):
+                zs[7, i] = fold_rows(k_slabs[i + 4])
+            give_field(7, 14)
         elif newton == 1:
-            give_fields(4, 2)
+            if j == 0:
+                give_field(3, 13)
+            give_field(4 + j, 13)
+
+    def end_fields(slabs, halo):
+        tall = [jnp.concatenate([slabs[s + 1], pltpu.roll(halo[0], 7 - 2 * s, 0)], axis=0) for s in range(4)]
+        wide = [
+            jnp.concatenate([slabs[s + 1], pltpu.roll(halo[1], LINE - 1 - 2 * s, 1)], axis=1) for s in range(4)
+        ]
+        return slabs, tall, wide
+
+    def end_means():
+        receive(8, 14)
+        slabs, tall, wide = end_fields([end_zs[4, i] for i in range(6)], [end_halo[4, i] for i in range(2)])
+        for i in range(5):
+            end_x[i] = mean_of(slabs[i], slabs[i + 1])
+        for s in range(4):
+            end_y[s] = mean_of(tall[s], up(tall[s], 0))
+            end_z[s] = mean_of(wide[s], up(wide[s], 1))
 
     for newton in range(NEWTON):
         coefficients()
@@ -469,7 +481,8 @@
                 pack_z([raw_h[f, 5 + s, 8:16] for f in range(3) for s in range(4)], 1)
                 exchange_wide(raw_h, zed_h, 1, 3, 3, 1)
             else:
-                give_fields(6, 1)
+                give_field(6, 13)
+                end_means()
 
         c = solve(global_sum(rows, newton, beside))
         if newton + 1 < NEWTON:
@@ -484,27 +497,24 @@
 
     last_r.wait()
     last_s.wait()
-    receive(21 + 14 + 28 + 14, 13)
-    last = []
-    for i in range(6):
-        total = end_zs[3, i]
-        for j in range(3):
-            total = total + c[j] * end_zs[4 + j, i]
-        last.append(total)
+    receive(8 * 4, 13)
+    near = []
+    for tiles in ([end_zs.at[:, i] for i in range(6)], [end_halo.at[:, i] for i in range(2)]):
+        for tile in tiles:
+            total = tile[0]
+            for j in range(3):
+                total = total + c[j] * tile[1 + j]
+            near.append(total)
+    last, tall, wide = end_fields(near[:6], near[6:])
     low_flux = None
     for s in range(-1, 4):
-        lower, upper = last[s + 1][own], last[s + 2][own]
-        flux, _ = face_terms(end_x[s + 1], upper - lower)
+        flux, _ = face_terms(end_x[s + 1], last[s + 2] - last[s + 1])
         if s >= 0:
-            mid = last[s + 1]
-            tall = mid[:, 0:LINE]
-            wide = mid[0:8, :]
-            ends[0, s] = lower
-            near_k = jnp.concatenate([end_y[s, 8:16], end_y[s, 0:8]], axis=0)
-            flux_y, _ = face_terms(near_k, up(tall, 0) - tall)
-            flux_z, _ = face_terms(end_z[s], up(wide, 1) - wide)
+            ends[0, s] = last[s + 1]
+            flux_y, _ = face_terms(end_y[s], up(tall[s], 0) - tall[s])
+            flux_z, _ = face_terms(end_z[s], up(wide[s], 1) - wide[s])
             ends[1, s] = (
-                end_rs[0, s] * lower
+                end_rs[0, s] * last[s + 1]
                 - (flux - low_flux)
                 - (flux_y - down(flux_y, 0))[0:8]
                 - (flux_z - down(flux_z, 1))[:, 0:LINE]
@@ -542,12 +552,12 @@
         vmem(13, *full), vmem(12, *full), vmem(12, *full), vmem(12, *full), vmem(12, *full),
         vmem(12, *half), vmem(8, *half), vmem(7, *half), vmem(6, *half), vmem(6, *half), vmem(6, *half), vmem(6, *half),
         vmem(6, *half), vmem(5, *half), vmem(4, *half), vmem(4, *half), vmem(4, *half), vmem(4, *half),
-        vmem(7, 6, *half), vmem(2, 3, 1, LINE), vmem(2, 1, 1, LINE), vmem(2, plane - 1, 1, LINE), vmem(2, line - 1, 1, LINE),
+        vmem(8, 6, *half), vmem(2, 3, 1, LINE), vmem(2, 1, 1, LINE), vmem(2, plane - 1, 1, LINE), vmem(2, line - 1, 1, LINE),
         vmem(2, 4, *tile), vmem(160, *tile),
-        vmem(7, 6, *half), vmem(5, *tile), vmem(4, 16, LINE), vmem(4, ROWS, 2 * LINE), vmem(2, 4, *tile),
-        pltpu.SemaphoreType.DMA((4,)), pltpu.SemaphoreType.DMA((14,)), pltpu.SemaphoreType.REGULAR,
+        vmem(5, 6, *tile), vmem(5, 2, *tile), vmem(5, 2, *tile), vmem(5, *tile), vmem(4, 16, LINE), vmem(4, ROWS, 2 * LINE), vmem(2, 4, *tile),
+        pltpu.SemaphoreType.DMA((4,)), pltpu.SemaphoreType.DMA((15,)), pltpu.SemaphoreType.REGULAR,
     ]
-    spec = pl.BlockSpec(memory_space=pl.ANY)
+    spec = pl.BlockSpec(memory_space=pltpu.MemorySpace.HBM)
     return pl.pallas_call(
         functools.partial(kernel, sizes),
         out_shape=[jax.ShapeDtypeStruct(state.shape, jnp.float32)] * 2,
@@ -555,7 +565,7 @@
         out_specs=[spec] * 2,
         scratch_shapes=scratch,
         compiler_params=pltpu.CompilerParams(
-            collective_id=0, has_side_effects=True, vmem_limit_bytes=32 * 1024 * 1024
+            collective_id=0, has_side_effects=True, vmem_limit_bytes=61 * 1024 * 1024
         ),
     )(state, conductivity, reaction, source)
 

time: 88.1 us -> 79.5 us (0.902)
  Pallas kernels: 82.9 us -> 76.7 us
  local copies, waits for them, and re-layouts: 4.07 us -> 1.94 us
    pallas_call x1, Pallas kernels: 82.9 us -> 76.7 us  [local(): pl.pallas_call(functools.partial(kernel, sizes), out_shape=[jax.ShapeDtyp...]
    unnamed x10 -> x4, local copies, waits for them, and re-layouts: 4.07 us -> 1.94 us
where the time goes in v4:
time: 79.5 us; the launch traced here: 79.3 us
  Pallas kernels  76.7 us (96%)
  local copies, waits for them, and re-layouts  1.94 us (2%)
    pallas_call x1, Pallas kernels, local(): pl.pallas_call(functools.partial(kernel, sizes), out_shape=[jax.ShapeDtyp...  76.7 us
    unnamed x4, local copies, waits for them, and re-layouts  1.94 us

profile of v4, /device:TPU:1, one launch (start us, length us, event | category | flops | bytes accessed | tf_op | source)
XLA Modules:
  0.0 79.3 jit_solution(7322506453249096041)
XLA Ops:
  0.6 76.7 %shard_map.59 = (f32[4,8,128]{2,1,0:T(8,128)}, f32[4,8,128]{2,1,0:T(8,128)}) custom-call(f32[4,8,128]{2,1,0:T(8,128)} %u_ref.1, f32[4,8,128]{2,1,0:T(8,128)} %k_ref.1, f32[4,8,128]{2,1,0:T(8,128)} %r_ref.1, f32[4,8,128]{2,1,0:T(8,128)} %s_ref.1), custom_call_target="tpu_custom_call" | custom-call | tf_op jit(solution)/shard_map/pallas_call | solution.py:561
  77.3 0.0 copy-start
  77.3 1.3 %copy.8 = f32[4,8,128]{2,1,0:T(8,128)} copy(f32[4,8,128]{2,1,0:T(8,128)} %get-tuple-element.4) | data formatting | bytes 32768
  78.7 0.0 copy-done
  78.7 0.6 copy.9
Async XLA Ops:
  77.3 1.3 %copy-start = (f32[4,8,128]{2,1,0:T(8,128)S(1)}, f32[4,8,128]{2,1,0:T(8,128)}, u32[]{:S(2)}) copy-start(f32[4,8,128]{2,1,0:T(8,128)} %get-tuple-element.5) | copy-start | bytes 49156

commit v5 on v4

--- a/solution.py
+++ b/solution.py
@@ -73,7 +73,7 @@
 
 def kernel(
     sizes, u_ref, k_ref, r_ref, s_ref, out_u, out_f,
-    raw0, zed0, raw_h, zed_h, raw_e, zed_e, pack, box_u, mean_x, mean_y, mean_z, react, src,
+    raw0, corner0, zed0, far0, raw_h, corner_h, zed_h, far_h, v_out, v_face, v_edge, pack, corner_pack, box_u, mean_x, mean_y, mean_z, react, src,
     v0, inv, wx, wyu, wyl, wzu, wzl, cinv, cwx, cwyu, cwyl, cwzu, cwzl, zs, sums, got1, got2, got3, ends, dummy,
     end_zs, end_pack, end_halo, end_x, end_y, end_z, end_rs, send_sem, recv_sem, far_sem,
 ):
@@ -106,11 +106,13 @@
         long_line.append(((there // ny) * 4 + lax.rem(mx, 4), lax.rem(there, ny), mz))
 
     offsets = [(dx, dy, dz) for dx in (-1, 0, 1) for dy in (-1, 0, 1) for dz in (-1, 0, 1)]
-    offsets = [d for d in offsets if d != (0, 0, 0)] + [(2, 0, 0), (-2, 0, 0)]
+    offsets = [d for d in offsets if d != (0, 0, 0)]
+    offsets += [(dx, 0, dz) for dx in (2, -2) for dz in (-1, 0, 1)]
 
     barrier = pltpu.get_barrier_semaphore()
     partners = [block_at(*d) for d in offsets]
-    far_ones = [(lax.rem(mx + 4, nx), my, mz), (lax.rem(mx + nx - 4, nx), my, mz)]
+    far_ones = [(lax.rem(mx + step, nx), my, mz) for step in (4, nx - 4)]
+    far_ones += [(mx, my, lax.rem(mz + step, nz)) for step in (2, nz - 2)]
 
     @pl.when(jnp.logical_not(alone))
     def _():
@@ -134,29 +136,47 @@
         pltpu.make_async_copy(part, part, recv_sem.at[slot]).wait()
 
     def pack_z(tiles, place):
-        low = jnp.zeros((ROWS, LINE), jnp.float32)
-        high = low
-        for g, tile in enumerate(tiles):
-            mine = lane // 8 == g
-            low = jnp.where(mine, tile if g == 0 else pltpu.roll(tile, 8 * g, 1), low)
-            shift = (8 * g + 8) % LINE
-            high = jnp.where(mine, pltpu.roll(tile, shift, 1) if shift else tile, high)
-        pack[place, 0] = low
-        pack[place, 1] = high
-
-    def unpack_z(low_tile, high_tile, g):
-        shift = (LINE - 8 * g) % LINE
-        above = pltpu.roll(low_tile, shift, 1) if shift else low_tile
-        shift = (LINE - 8 - 8 * g) % LINE
-        below = pltpu.roll(high_tile, shift, 1) if shift else high_tile
+        for t in range(0, len(tiles), 8):
+            low = jnp.zeros((ROWS, LINE), jnp.float32)
+            high = low
+            for g, tile in enumerate(tiles[t : t + 8]):
+                mine = lane // 16 == g
+                low = jnp.where(mine, tile if g == 0 else pltpu.roll(tile, 16 * g, 1), low)
+                shift = (16 * g + 16) % LINE
+                high = jnp.where(mine, pltpu.roll(tile, shift, 1) if shift else tile, high)
+            pack[place, 0, t // 8] = low
+            pack[place, 1, t // 8] = high
+
+    def unpack_z(low_tiles, high_tiles, g):
+        t, g = divmod(g, 8)
+        shift = (LINE - 16 * g) % LINE
+        above = pltpu.roll(low_tiles[t], shift, 1) if shift else low_tiles[t]
+        shift = (LINE - 16 - 16 * g) % LINE
+        below = pltpu.roll(high_tiles[t], shift, 1) if shift else high_tiles[t]
         return jnp.where(lane < 64, above, below)
 
-    def exchange_wide(raw, zed, place, fields, far, slot):
+    def pack_corners(raw, place, fields):
+        low_rows = index_of((ROWS, LINE), 0) < 4
+        for f in range(fields):
+            for pair in range(2):
+                one, two = raw[f, 5 + 2 * pair, 8:16], raw[f, 6 + 2 * pair, 8:16]
+                two = pltpu.roll(two, 4, 0)
+                corner_pack[place, 1, f, pair] = jnp.where(low_rows, two, one)
+                corner_pack[place, 0, f, pair] = jnp.where(low_rows, one, two)
+
+    def exchange_wide(raw, corner, zed, zed2, place, fields, far, slot):
         everything = pl.ds(0, fields)
         own = (everything, pl.ds(5, 4), pl.ds(8, 8))
-        for dx, dy in CORNERS:
-            target = (everything, pl.ds(5 - 4 * dx, 4), pl.ds(8 - 8 * dy, 8))
-            send(raw.at[own], raw.at[target], slot, block_at(dx, dy, 0))
+        rows = pl.ds(8, 8)
+        far_tiles = pl.ds(0, (far + 1) // 2)
+        for dx in (2, -2):
+            for dz in (1, -1):
+                send(
+                    pack.at[place, (1 + dz) // 2, far_tiles],
+                    zed2.at[(2 - dx) // 4, (1 - dz) // 2, far_tiles],
+                    slot,
+                    block_at(dx, 0, dz),
+                )
         for dx, dy in CORNERS + CROSS:
             for dz in (1, -1):
                 send(
@@ -165,69 +185,93 @@
                     slot,
                     block_at(dx, dy, dz),
                 )
+        for dx, dy in CORNERS:
+            send(
+                corner_pack.at[place, (1 + dy) // 2, everything],
+                corner.at[(1 - dx) // 2, (1 - dy) // 2, everything],
+                slot,
+                block_at(dx, dy, 0),
+            )
         some = pl.ds(0, far)
-        rows = pl.ds(8, 8)
         send(raw.at[some, pl.ds(8, 1), rows], raw.at[some, pl.ds(0, 1), rows], slot, block_at(2, 0, 0))
         send(raw.at[some, pl.ds(5, 1), rows], raw.at[some, pl.ds(13, 1), rows], slot, block_at(-2, 0, 0))
         for dx, dy in CROSS[1:]:
             target = (everything, pl.ds(5 - 4 * dx, 4), pl.ds(8 - 8 * dy, 8))
             send(raw.at[own], raw.at[target], slot, block_at(dx, dy, 0))
-        return 16 * fields + 18 + 2 * far + 16 * fields
-
-    def wide_slab(raw, zed, field, i):
+        return wide_tiles(fields, far)
+
+    def wide_tiles(fields, far):
+        return 4 * ((far + 1) // 2) + 36 + 8 * fields + 2 * far + 16 * fields
+
+    nothing = jnp.zeros((ROWS, LINE), jnp.float32)
+
+    def wide_slab(raw, corner, zed, zed2, field, i):
         if i in (0, 13):
-            nothing = jnp.zeros((ROWS, LINE), jnp.float32)
-            main = jnp.concatenate([nothing, raw[field, i, 8:16], nothing], axis=0)
-            return jnp.concatenate([main, jnp.zeros_like(main)], axis=1)
-        main = raw[field, i]
+            side, s = (0, 3) if i == 0 else (1, 0)
+            halo = unpack_z(zed2[side, 1], zed2[side, 0], field * 4 + s)
+            mid = jnp.concatenate([raw[field, i, 8:16], halo], axis=1)
+            empty = jnp.zeros_like(mid)
+            return jnp.concatenate([empty, mid, empty], axis=0)
         column, s = divmod(i - 1, 4)
+        if column == 1:
+            main = raw[field, i]
+        else:
+            ends_y = []
+            for y in range(2):
+                packed = corner[column // 2, y, field, s // 2]
+                ends_y.append(pltpu.roll(packed, 4, 0) if s % 2 else packed)
+            main = jnp.concatenate([ends_y[0], raw[field, i, 8:16], ends_y[1]], axis=0)
         g = field * 4 + s
         halo = [unpack_z(zed[column, y, 1], zed[column, y, 0], g) for y in range(3)]
         return jnp.concatenate([main, jnp.concatenate(halo, axis=0)], axis=1)
 
     def exchange_v(tiles, e, between):
-        place, slot = 2 + e, 2 + e
+        slot = 2 + e
+        packed = nothing
         for s in range(4):
-            raw_e[e, 4 + s, 8:16] = tiles[s]
-        pack_z(tiles, place)
-        raw, zed = raw_e.at[e], zed_e.at[e]
-        rows = pl.ds(8, 8)
+            v_out[e, 1 + s] = tiles[s][:, 0:LINE]
+            part = pltpu.roll(tiles[s][:, LINE : 2 * LINE], 16 * s + 8, 1)
+            packed = jnp.where(lane // 16 == s, part, packed)
+        v_out[e, 0] = packed
+        v_out[e, 5] = packed
         for dx, dy in CORNERS:
-            source = (pl.ds(6 if dx > 0 else 4, 2), rows)
-            target = (pl.ds(2 if dx > 0 else 8, 2), pl.ds(8 - 8 * dy, 8))
-            send(raw.at[source], raw.at[target], slot, block_at(dx, dy, 0))
-        for dx, dy in CROSS:
-            for dz in (1, -1):
-                send(
-                    pack.at[place, (1 + dz) // 2],
-                    zed.at[1 - dx, 1 - dy, (1 - dz) // 2],
-                    slot,
-                    block_at(dx, dy, dz),
-                )
-        for dx, dy in CROSS[1:]:
-            target = (pl.ds(4 - 4 * dx, 4), pl.ds(8 - 8 * dy, 8))
-            send(raw.at[pl.ds(4, 4), rows], raw.at[target], slot, block_at(dx, dy, 0))
+            send(
+                v_out.at[e, pl.ds(3 if dx > 0 else 0, 3)],
+                v_edge.at[e, (1 - dx) // 2, (1 - dy) // 2],
+                slot,
+                block_at(dx, dy, 0),
+            )
+        for n, (dx, dy) in enumerate(CROSS[1:]):
+            send(v_out.at[e, pl.ds(1, 5)], v_face.at[e, n], slot, block_at(dx, dy, 0))
         between()
-        receive(8 + 10 + 16, slot)
+        receive(12 + 20, slot)
+        row = index_of((ROWS, LINE), 0)
+
+        def spread(zeds, s):
+            return pltpu.roll(zeds, LINE - 8 - 16 * s, 1)
+
         slabs = []
-        nothing = jnp.zeros((ROWS, LINE), jnp.float32)
-        row = index_of((ROWS, LINE), 0)
         for i in range(12):
-            if 2 <= i < 10:
-                main = fold_rows(raw_e[e, i])
+            column, s = divmod(i, 4)
+            if column == 1:
+                mid = tiles[s]
+                side = [
+                    jnp.where(row < 4, v_face[e, 3, s], v_face[e, 2, s]),
+                    jnp.where(row < 4, spread(v_face[e, 3, 4], s), spread(v_face[e, 2, 4], s)),
+                ]
             else:
-                main = jnp.concatenate([raw_e[e, i, 8:16], nothing], axis=0)
-            column, s = divmod(i, 4)
-            own_halo, side_halo = nothing, nothing
-            if 2 <= i < 10:
-                own_halo = unpack_z(zed_e[e, column, 1, 1], zed_e[e, column, 1, 0], s)
-            if 4 <= i < 8:
-                side_halo = jnp.where(
-                    row < 4,
-                    unpack_z(zed_e[e, 1, 2, 1], zed_e[e, 1, 2, 0], s),
-                    unpack_z(zed_e[e, 1, 0, 1], zed_e[e, 1, 0, 0], s),
-                )
-            slabs.append(jnp.concatenate([main, jnp.concatenate([own_halo, side_halo], axis=0)], axis=1))
+                face = 0 if column == 0 else 1
+                mid = jnp.concatenate([v_face[e, face, s], spread(v_face[e, face, 4], s)], axis=1)
+                side = [nothing, nothing]
+                if 2 <= i < 10:
+                    at = s - 2 if column == 0 else s + 1
+                    z_at = 2 if column == 0 else 0
+                    low, high = v_edge.at[e, face, 0], v_edge.at[e, face, 1]
+                    side = [
+                        jnp.where(row < 4, high[at], low[at]),
+                        jnp.where(row < 4, spread(high[z_at], s), spread(low[z_at], s)),
+                    ]
+            slabs.append(jnp.concatenate([mid, jnp.concatenate(side, axis=1)], axis=0))
         return slabs
 
     def coefficients():
@@ -309,18 +353,16 @@
 
     def image(j, s):
         i = s + 1
-        mid = zs[j, i]
-        here = mid[0:8, 0:LINE]
-        tall, wide = mid[:, 0:LINE], mid[0:8, :]
-        own = (slice(0, 8), slice(0, LINE))
-        total = react[i + 3, 8:16, 0:LINE] * here
+        tall = zs[j, i]
+        here = tall[0:8]
+        total = react[i + 3, 8:16] * here
         for weight, other in (
-            (wx[(i,) + own], zs[(j, i - 1) + own]),
-            (wx[(i + 1,) + own], zs[(j, i + 1) + own]),
-            (wyu[(i,) + own], up(tall, 0)[0:8]),
-            (wyl[(i,) + own], down(tall, 0)[0:8]),
-            (wzu[(i,) + own], up(wide, 1)[:, 0:LINE]),
-            (wzl[(i,) + own], down(wide, 1)[:, 0:LINE]),
+            (wx[i, 0:8], zs[j, i - 1, 0:8]),
+            (wx[i + 1, 0:8], zs[j, i + 1, 0:8]),
+            (wyu[i, 0:8], up(tall, 0)[0:8]),
+            (wyl[i, 0:8], down(tall, 0)[0:8]),
+            (wzu[i, 0:8], up(here, 1)),
+            (wzl[i, 0:8], down(here, 1)),
         ):
             total = total + weight * (here - other)
         return total
@@ -335,14 +377,14 @@
             mixed = jnp.where(group == n, row, mixed)
         phases = ((core_line, got1), (plane_line, got2), (long_line, got3))
         for phase, (partners, got) in enumerate(phases):
+            if phase == 1 and which == 0:
+                pl.semaphore_wait(far_sem, 4)
             sums[which, phase] = mixed
             slot = 6 + 3 * which + phase
             for n, partner in enumerate(partners):
                 send(sums.at[which, phase], got.at[which, n], slot, partner)
             if phase == 0:
                 between()
-            if phase == 1 and which == 0:
-                pl.semaphore_wait(far_sem, 2)
             part = got.at[which]
             pltpu.make_async_copy(part, part, recv_sem.at[slot]).wait()
             mixed = mixed + jnp.sum(got[which], axis=0)
@@ -370,9 +412,9 @@
         return c0, c1, c2
 
     def total_of(tiles, others):
-        total = tiles[0] * others[0]
+        total = tiles[0][:, 0:LINE] * others[0]
         for s in range(1, 4):
-            total = total + tiles[s] * others[s]
+            total = total + tiles[s][:, 0:LINE] * others[s]
         return total
 
     given = []
@@ -400,21 +442,22 @@
     last_s.start()
     receive(16, 12)
     pack_z([raw0[f, 5 + s, 8:16] for f in range(4) for s in range(4)], 0)
-    count = exchange_wide(raw0, zed0, 0, 4, 2, 0)
+    pack_corners(raw0, 0, 4)
+    count = exchange_wide(raw0, corner0, zed0, far0, 0, 4, 2, 0)
     receive(count, 0)
     for other in far_ones:
         pl.semaphore_signal(far_sem, inc=1, device_id=other, device_id_type=MESH)
     for i in range(14):
-        box_u[i] = wide_slab(raw0, zed0, 0, i)
-    k_slabs = [wide_slab(raw0, zed0, 1, i) for i in range(14)]
+        box_u[i] = wide_slab(raw0, corner0, zed0, far0, 0, i)
+    k_slabs = [wide_slab(raw0, corner0, zed0, far0, 1, i) for i in range(14)]
     for i in range(13):
         mean_x[i] = mean_of(k_slabs[i], k_slabs[i + 1])
     for i in range(12):
         k = k_slabs[i + 1]
         mean_y[i] = mean_of(k, up(k, 0))
         mean_z[i] = mean_of(k, up(k, 1))
-        react[i] = wide_slab(raw0, zed0, 2, i + 1)
-        src[i] = wide_slab(raw0, zed0, 3, i + 1)
+        react[i] = wide_slab(raw0, corner0, zed0, far0, 2, i + 1)
+        src[i] = wide_slab(raw0, corner0, zed0, far0, 3, i + 1)
 
     own = (slice(0, 8), slice(0, LINE))
 
@@ -462,7 +505,7 @@
         coefficients()
         rows = []
         v = [v0[i] for i in range(12)]
-        tiles = [slab[0:8, 0:LINE] for slab in v[4:8]]
+        tiles = [slab[0:8] for slab in v[4:8]]
         for j in range(KRYLOV):
             at = 4 * newton + j
             precondition(v, at)
@@ -479,18 +522,19 @@
         def beside(newton=newton):
             if newton + 1 < NEWTON:
                 pack_z([raw_h[f, 5 + s, 8:16] for f in range(3) for s in range(4)], 1)
-                exchange_wide(raw_h, zed_h, 1, 3, 3, 1)
+                pack_corners(raw_h, 1, 3)
+                exchange_wide(raw_h, corner_h, zed_h, far_h, 1, 3, 3, 1)
             else:
                 give_field(6, 13)
                 end_means()
 
         c = solve(global_sum(rows, newton, beside))
         if newton + 1 < NEWTON:
-            receive(32 * 3 + 18 + 6, 1)
+            receive(wide_tiles(3, 3), 1)
             for i in range(14):
                 total = box_u[i]
                 for j in range(3):
-                    total = total + c[j] * wide_slab(raw_h, zed_h, j, i)
+                    total = total + c[j] * wide_slab(raw_h, corner_h, zed_h, far_h, j, i)
                 box_u[i] = total
                 if 4 <= i < 10:
                     zs[3, i - 4] = fold_rows(total)
@@ -547,8 +591,9 @@
     full, half = (24, 2 * LINE), (16, 2 * LINE)
     tile = (ROWS, LINE)
     scratch = [
-        vmem(4, 14, 24, LINE), vmem(3, 3, 2, *tile), vmem(3, 14, 24, LINE), vmem(3, 3, 2, *tile),
-        vmem(4, 12, 24, LINE), vmem(4, 3, 3, 2, *tile), vmem(6, 2, *tile), vmem(14, *full),
+        vmem(4, 14, 24, LINE), vmem(2, 2, 4, 2, *tile), vmem(3, 3, 2, 2, *tile), vmem(2, 2, 2, *tile),
+        vmem(3, 14, 24, LINE), vmem(2, 2, 3, 2, *tile), vmem(3, 3, 2, 2, *tile), vmem(2, 2, 2, *tile),
+        vmem(4, 6, *tile), vmem(4, 4, 5, *tile), vmem(4, 2, 2, 3, *tile), vmem(2, 2, 2, *tile), vmem(2, 2, 4, 2, *tile), vmem(14, *full),
         vmem(13, *full), vmem(12, *full), vmem(12, *full), vmem(12, *full), vmem(12, *full),
         vmem(12, *half), vmem(8, *half), vmem(7, *half), vmem(6, *half), vmem(6, *half), vmem(6, *half), vmem(6, *half),
         vmem(6, *half), vmem(5, *half), vmem(4, *half), vmem(4, *half), vmem(4, *half), vmem(4, *half),

time: 79.5 us -> 80.8 us (1.016)
  Pallas kernels: 76.7 us -> 78 us
    pallas_call x1, Pallas kernels: 76.7 us -> 78 us  [local(): pl.pallas_call(functools.partial(kernel, sizes), out_shape=[jax.ShapeDtyp...]
where the time goes in v5:
time: 80.8 us; the launch traced here: 80.6 us
  Pallas kernels  78 us (97%)
  local copies, waits for them, and re-layouts  1.94 us (2%)
    pallas_call x1, Pallas kernels, local(): pl.pallas_call(functools.partial(kernel, sizes), out_shape=[jax.ShapeDtyp...  78 us
    unnamed x4, local copies, waits for them, and re-layouts  1.94 us

profile of v5, /device:TPU:1, one launch (start us, length us, event | category | flops | bytes accessed | tf_op | source)
XLA Modules:
  0.0 80.6 jit_solution(1005592801140332217)
XLA Ops:
  0.6 78.0 %shard_map.59 = (f32[4,8,128]{2,1,0:T(8,128)}, f32[4,8,128]{2,1,0:T(8,128)}) custom-call(f32[4,8,128]{2,1,0:T(8,128)} %u_ref.1, f32[4,8,128]{2,1,0:T(8,128)} %k_ref.1, f32[4,8,128]{2,1,0:T(8,128)} %r_ref.1, f32[4,8,128]{2,1,0:T(8,128)} %s_ref.1), custom_call_target="tpu_custom_call" | custom-call | tf_op jit(solution)/shard_map/pallas_call | solution.py:606
  78.7 0.0 copy-start
  78.7 1.3 %copy.8 = f32[4,8,128]{2,1,0:T(8,128)} copy(f32[4,8,128]{2,1,0:T(8,128)} %get-tuple-element.4) | data formatting | bytes 32768
  80.0 0.0 copy-done
  80.0 0.6 copy.9
Async XLA Ops:
  78.7 1.3 %copy-start = (f32[4,8,128]{2,1,0:T(8,128)S(1)}, f32[4,8,128]{2,1,0:T(8,128)}, u32[]{:S(2)}) copy-start(f32[4,8,128]{2,1,0:T(8,128)} %get-tuple-element.5) | copy-start | bytes 49156

commit v6 on v5

--- a/solution.py
+++ b/solution.py
@@ -72,9 +72,9 @@
 
 
 def kernel(
-    sizes, u_ref, k_ref, r_ref, s_ref, out_u, out_f,
+    sizes, u_ref, k_ref, r_ref, s_ref, out,
     raw0, corner0, zed0, far0, raw_h, corner_h, zed_h, far_h, v_out, v_face, v_edge, pack, corner_pack, box_u, mean_x, mean_y, mean_z, react, src,
-    v0, inv, wx, wyu, wyl, wzu, wzl, cinv, cwx, cwyu, cwyl, cwzu, cwzl, zs, sums, got1, got2, got3, ends, dummy,
+    v0, inv, wx, wyu, wyl, wzu, wzl, cinv, cwx, cwyu, cwyl, cwzu, cwzl, zs, sums, got1, got2, got3, dummy,
     end_zs, end_pack, end_halo, end_x, end_y, end_z, end_rs, send_sem, recv_sem, far_sem,
 ):
     nx, ny, nz = sizes
@@ -135,17 +135,16 @@
         part = dummy.at[pl.ds(0, tiles)]
         pltpu.make_async_copy(part, part, recv_sem.at[slot]).wait()
 
-    def pack_z(tiles, place):
-        for t in range(0, len(tiles), 8):
-            low = jnp.zeros((ROWS, LINE), jnp.float32)
-            high = low
-            for g, tile in enumerate(tiles[t : t + 8]):
-                mine = lane // 16 == g
-                low = jnp.where(mine, tile if g == 0 else pltpu.roll(tile, 16 * g, 1), low)
-                shift = (16 * g + 16) % LINE
-                high = jnp.where(mine, pltpu.roll(tile, shift, 1) if shift else tile, high)
-            pack[place, 0, t // 8] = low
-            pack[place, 1, t // 8] = high
+    def pack_z(tiles, place, at):
+        low = jnp.zeros((ROWS, LINE), jnp.float32)
+        high = low
+        for g, tile in enumerate(tiles):
+            mine = lane // 16 == g
+            low = jnp.where(mine, tile if g == 0 else pltpu.roll(tile, 16 * g, 1), low)
+            shift = (16 * g + 16) % LINE
+            high = jnp.where(mine, pltpu.roll(tile, shift, 1) if shift else tile, high)
+        pack[place, 0, at] = low
+        pack[place, 1, at] = high
 
     def unpack_z(low_tiles, high_tiles, g):
         t, g = divmod(g, 8)
@@ -155,28 +154,49 @@
         below = pltpu.roll(high_tiles[t], shift, 1) if shift else high_tiles[t]
         return jnp.where(lane < 64, above, below)
 
-    def pack_corners(raw, place, fields):
+    def pack_corners(raw, place, first, fields):
         low_rows = index_of((ROWS, LINE), 0) < 4
-        for f in range(fields):
+        for f in range(first, first + fields):
             for pair in range(2):
                 one, two = raw[f, 5 + 2 * pair, 8:16], raw[f, 6 + 2 * pair, 8:16]
                 two = pltpu.roll(two, 4, 0)
                 corner_pack[place, 1, f, pair] = jnp.where(low_rows, two, one)
                 corner_pack[place, 0, f, pair] = jnp.where(low_rows, one, two)
 
-    def exchange_wide(raw, corner, zed, zed2, place, fields, far, slot):
-        everything = pl.ds(0, fields)
-        own = (everything, pl.ds(5, 4), pl.ds(8, 8))
-        rows = pl.ds(8, 8)
-        far_tiles = pl.ds(0, (far + 1) // 2)
+    def exchange_wide(raw, corner, place, first, fields, all_pairs, slot):
+        which = pl.ds(first, fields)
+        own = (which, pl.ds(5, 4), pl.ds(8, 8))
+        for dx, dy in CROSS[1:3]:
+            target = (which, pl.ds(5 - 4 * dx, 4), pl.ds(8 - 8 * dy, 8))
+            send(raw.at[own], raw.at[target], slot, block_at(dx, dy, 0))
+        for dx, dy in CORNERS:
+            pairs = pl.ds(0, 2) if all_pairs else pl.ds((1 + dx) // 2, 1)
+            send(
+                corner_pack.at[place, (1 + dy) // 2, which, pairs],
+                corner.at[(1 - dx) // 2, (1 - dy) // 2, which, pairs],
+                slot,
+                block_at(dx, dy, 0),
+            )
+        for dx, dy in CROSS[3:]:
+            target = (which, pl.ds(5 - 4 * dx, 4), pl.ds(8 - 8 * dy, 8))
+            send(raw.at[own], raw.at[target], slot, block_at(dx, dy, 0))
+        return 16 * fields + (8 if all_pairs else 4) * fields
+
+    def exchange_far(raw, zed2, place, fields, slot):
+        some, rows, tiles = pl.ds(0, fields), pl.ds(8, 8), (fields + 1) // 2
+        send(raw.at[some, pl.ds(8, 1), rows], raw.at[some, pl.ds(0, 1), rows], slot, block_at(2, 0, 0))
+        send(raw.at[some, pl.ds(5, 1), rows], raw.at[some, pl.ds(13, 1), rows], slot, block_at(-2, 0, 0))
         for dx in (2, -2):
             for dz in (1, -1):
                 send(
-                    pack.at[place, (1 + dz) // 2, far_tiles],
-                    zed2.at[(2 - dx) // 4, (1 - dz) // 2, far_tiles],
+                    pack.at[place, (1 + dz) // 2, pl.ds(0, tiles)],
+                    zed2.at[(2 - dx) // 4, (1 - dz) // 2, pl.ds(0, tiles)],
                     slot,
                     block_at(dx, 0, dz),
                 )
+        return 2 * fields + 4 * tiles
+
+    def exchange_z(zed, place, slot):
         for dx, dy in CORNERS + CROSS:
             for dz in (1, -1):
                 send(
@@ -185,30 +205,16 @@
                     slot,
                     block_at(dx, dy, dz),
                 )
-        for dx, dy in CORNERS:
-            send(
-                corner_pack.at[place, (1 + dy) // 2, everything],
-                corner.at[(1 - dx) // 2, (1 - dy) // 2, everything],
-                slot,
-                block_at(dx, dy, 0),
-            )
-        some = pl.ds(0, far)
-        send(raw.at[some, pl.ds(8, 1), rows], raw.at[some, pl.ds(0, 1), rows], slot, block_at(2, 0, 0))
-        send(raw.at[some, pl.ds(5, 1), rows], raw.at[some, pl.ds(13, 1), rows], slot, block_at(-2, 0, 0))
-        for dx, dy in CROSS[1:]:
-            target = (everything, pl.ds(5 - 4 * dx, 4), pl.ds(8 - 8 * dy, 8))
-            send(raw.at[own], raw.at[target], slot, block_at(dx, dy, 0))
-        return wide_tiles(fields, far)
-
-    def wide_tiles(fields, far):
-        return 4 * ((far + 1) // 2) + 36 + 8 * fields + 2 * far + 16 * fields
+        return 36
 
     nothing = jnp.zeros((ROWS, LINE), jnp.float32)
 
-    def wide_slab(raw, corner, zed, zed2, field, i):
-        if i in (0, 13):
-            side, s = (0, 3) if i == 0 else (1, 0)
-            halo = unpack_z(zed2[side, 1], zed2[side, 0], field * 4 + s)
+    def wide_slab(raw, corner, zed, zed2, field, i, slim=False):
+        outer = i in (0, 13)
+        if outer or (slim and i in (1, 2, 11, 12)):
+            column, s = ((i - 1) // 4, (i - 1) % 4) if not outer else (0, 3) if i == 0 else (1, 0)
+            low, high = (zed2[column, 1], zed2[column, 0]) if outer else (zed[column, 1, 1], zed[column, 1, 0])
+            halo = unpack_z(low, high, field * 4 + s)
             mid = jnp.concatenate([raw[field, i, 8:16], halo], axis=1)
             empty = jnp.zeros_like(mid)
             return jnp.concatenate([empty, mid, empty], axis=0)
@@ -383,7 +389,7 @@
             slot = 6 + 3 * which + phase
             for n, partner in enumerate(partners):
                 send(sums.at[which, phase], got.at[which, n], slot, partner)
-            if phase == 0:
+            if phase == 1:
                 between()
             part = got.at[which]
             pltpu.make_async_copy(part, part, recv_sem.at[slot]).wait()
@@ -435,15 +441,23 @@
         given.append(tiles)
 
     pl.semaphore_wait(barrier, len(partners) + 1 - alone.astype(jnp.int32))
-    give([u_ref, k_ref, r_ref, s_ref], [raw0.at[f, pl.ds(5, 4), pl.ds(8, 8)] for f in range(4)], 12, 16)
+    homes = [raw0.at[f, pl.ds(5, 4), pl.ds(8, 8)] for f in range(4)]
+    give([u_ref, k_ref], homes[:2], 12, 8)
+    give([r_ref, s_ref], homes[2:], 15, 8)
     last_r = pltpu.make_async_copy(r_ref, end_rs.at[0], send_sem.at[2])
     last_s = pltpu.make_async_copy(s_ref, end_rs.at[1], send_sem.at[3])
     last_r.start()
     last_s.start()
-    receive(16, 12)
-    pack_z([raw0[f, 5 + s, 8:16] for f in range(4) for s in range(4)], 0)
-    pack_corners(raw0, 0, 4)
-    count = exchange_wide(raw0, corner0, zed0, far0, 0, 4, 2, 0)
+    receive(8, 12)
+    pack_corners(raw0, 0, 0, 2)
+    count = exchange_wide(raw0, corner0, 0, 0, 2, True, 0)
+    pack_z([raw0[f, 5 + s, 8:16] for f in range(2) for s in range(4)], 0, 0)
+    count += exchange_far(raw0, far0, 0, 2, 0)
+    receive(8, 15)
+    pack_corners(raw0, 0, 2, 2)
+    count += exchange_wide(raw0, corner0, 0, 2, 2, False, 0)
+    pack_z([raw0[f, 5 + s, 8:16] for f in range(2, 4) for s in range(4)], 0, 1)
+    count += exchange_z(zed0, 0, 0)
     receive(count, 0)
     for other in far_ones:
         pl.semaphore_signal(far_sem, inc=1, device_id=other, device_id_type=MESH)
@@ -456,8 +470,8 @@
         k = k_slabs[i + 1]
         mean_y[i] = mean_of(k, up(k, 0))
         mean_z[i] = mean_of(k, up(k, 1))
-        react[i] = wide_slab(raw0, corner0, zed0, far0, 2, i + 1)
-        src[i] = wide_slab(raw0, corner0, zed0, far0, 3, i + 1)
+        react[i] = wide_slab(raw0, corner0, zed0, far0, 2, i + 1, True)
+        src[i] = wide_slab(raw0, corner0, zed0, far0, 3, i + 1, True)
 
     own = (slice(0, 8), slice(0, LINE))
 
@@ -519,18 +533,23 @@
             if j + 1 < KRYLOV:
                 v = exchange_v(tiles, 2 * newton + j, functools.partial(beside_v, newton, j))
 
-        def beside(newton=newton):
+        counts = []
+
+        def beside(newton=newton, counts=counts):
             if newton + 1 < NEWTON:
-                pack_z([raw_h[f, 5 + s, 8:16] for f in range(3) for s in range(4)], 1)
-                pack_corners(raw_h, 1, 3)
-                exchange_wide(raw_h, corner_h, zed_h, far_h, 1, 3, 3, 1)
+                pack_corners(raw_h, 1, 0, 3)
+                counts.append(exchange_wide(raw_h, corner_h, 1, 0, 3, True, 1))
+                pack_z([raw_h[f, 5 + s, 8:16] for f in range(2) for s in range(4)], 1, 0)
+                pack_z([raw_h[2, 5 + s, 8:16] for s in range(4)], 1, 1)
+                counts.append(exchange_far(raw_h, far_h, 1, 3, 1))
+                counts.append(exchange_z(zed_h, 1, 1))
             else:
                 give_field(6, 13)
                 end_means()
 
         c = solve(global_sum(rows, newton, beside))
         if newton + 1 < NEWTON:
-            receive(wide_tiles(3, 3), 1)
+            receive(sum(counts), 1)
             for i in range(14):
                 total = box_u[i]
                 for j in range(3):
@@ -554,10 +573,10 @@
     for s in range(-1, 4):
         flux, _ = face_terms(end_x[s + 1], last[s + 2] - last[s + 1])
         if s >= 0:
-            ends[0, s] = last[s + 1]
+            out[0, s] = last[s + 1]
             flux_y, _ = face_terms(end_y[s], up(tall[s], 0) - tall[s])
             flux_z, _ = face_terms(end_z[s], up(wide[s], 1) - wide[s])
-            ends[1, s] = (
+            out[1, s] = (
                 end_rs[0, s] * last[s + 1]
                 - (flux - low_flux)
                 - (flux_y - down(flux_y, 0))[0:8]
@@ -565,10 +584,6 @@
                 - end_rs[1, s]
             )
         low_flux = flux
-    store_u = pltpu.make_async_copy(ends.at[0], out_u, send_sem.at[2])
-    store_f = pltpu.make_async_copy(ends.at[1], out_f, send_sem.at[3])
-    store_u.start()
-    store_f.start()
     for copy in copies:
         copy.wait_send()
 
@@ -576,9 +591,6 @@
     def _():
         part = dummy.at[pl.ds(0, sum(given))]
         pltpu.make_async_copy(part, part, send_sem.at[1]).wait()
-
-    store_u.wait()
-    store_f.wait()
 
 
 def local(sizes, state, conductivity, reaction, source):
@@ -598,21 +610,22 @@
         vmem(12, *half), vmem(8, *half), vmem(7, *half), vmem(6, *half), vmem(6, *half), vmem(6, *half), vmem(6, *half),
         vmem(6, *half), vmem(5, *half), vmem(4, *half), vmem(4, *half), vmem(4, *half), vmem(4, *half),
         vmem(8, 6, *half), vmem(2, 3, 1, LINE), vmem(2, 1, 1, LINE), vmem(2, plane - 1, 1, LINE), vmem(2, line - 1, 1, LINE),
-        vmem(2, 4, *tile), vmem(160, *tile),
+        vmem(160, *tile),
         vmem(5, 6, *tile), vmem(5, 2, *tile), vmem(5, 2, *tile), vmem(5, *tile), vmem(4, 16, LINE), vmem(4, ROWS, 2 * LINE), vmem(2, 4, *tile),
-        pltpu.SemaphoreType.DMA((4,)), pltpu.SemaphoreType.DMA((15,)), pltpu.SemaphoreType.REGULAR,
+        pltpu.SemaphoreType.DMA((4,)), pltpu.SemaphoreType.DMA((16,)), pltpu.SemaphoreType.REGULAR,
     ]
     spec = pl.BlockSpec(memory_space=pltpu.MemorySpace.HBM)
-    return pl.pallas_call(
+    both = pl.pallas_call(
         functools.partial(kernel, sizes),
-        out_shape=[jax.ShapeDtypeStruct(state.shape, jnp.float32)] * 2,
+        out_shape=jax.ShapeDtypeStruct((2, *state.shape), jnp.float32),
         in_specs=[spec] * 4,
-        out_specs=[spec] * 2,
+        out_specs=pl.BlockSpec(memory_space=pltpu.VMEM),
         scratch_shapes=scratch,
         compiler_params=pltpu.CompilerParams(
             collective_id=0, has_side_effects=True, vmem_limit_bytes=61 * 1024 * 1024
         ),
     )(state, conductivity, reaction, source)
+    return both[0], both[1]
 
 
 def solution(mesh):

time: 80.8 us -> 79.3 us (0.981)
  Pallas kernels: 78 us -> 77 us
    unnamed x4 -> x0, local copies, waits for them, and re-layouts: 1.94 us -> none
    squeeze x0 -> x1, local copies, waits for them, and re-layouts: none -> 1.35 us  [local(): return (both[0], both[1])]
    pallas_call x1, Pallas kernels: 78 us -> 77 us  [local(): pl.pallas_call(functools.partial(kernel, sizes), out_shape=jax.ShapeDtype...]
where the time goes in v6:
time: 79.3 us; the launch traced here: 79 us
  Pallas kernels  77 us (97%)
  local copies, waits for them, and re-layouts  1.35 us (2%)
    pallas_call x1, Pallas kernels, local(): pl.pallas_call(functools.partial(kernel, sizes), out_shape=jax.ShapeDtype...  77 us

profile of v6, /device:TPU:1, one launch (start us, length us, event | category | flops | bytes accessed | tf_op | source)
XLA Modules:
  0.0 79.0 jit_solution(14266357760980328977)
XLA Ops:
  0.6 77.0 %shard_map.59 = f32[2,4,8,128]{3,2,1,0:T(8,128)} custom-call(f32[4,8,128]{2,1,0:T(8,128)} %u_ref.1, f32[4,8,128]{2,1,0:T(8,128)} %k_ref.1, f32[4,8,128]{2,1,0:T(8,128)} %r_ref.1, f32[4,8,128]{2,1,0:T(8,128)} %s_ref.1), custom_call_target="tpu_custom_call" | custom-call | tf_op jit(solution)/shard_map/pallas_call | solution.py:618
  77.7 1.3 %slice_bitcast_fusion = (f32[4,8,128]{2,1,0:T(8,128)}, f32[4,8,128]{2,1,0:T(8,128)}) fusion(f32[2,4,8,128]{3,2,1,0:T(8,128)} %shard_map.59), kind=kLoop, calls=%fused_computation | loop fusion | bytes 65536 | tf_op jit(solution)/shard_map/squeeze | solution.py:628

commit v7 on v6

--- a/solution.py
+++ b/solution.py
@@ -74,7 +74,7 @@
 def kernel(
     sizes, u_ref, k_ref, r_ref, s_ref, out,
     raw0, corner0, zed0, far0, raw_h, corner_h, zed_h, far_h, v_out, v_face, v_edge, pack, corner_pack, box_u, mean_x, mean_y, mean_z, react, src,
-    v0, inv, wx, wyu, wyl, wzu, wzl, cinv, cwx, cwyu, cwyl, cwzu, cwzl, zs, sums, got1, got2, got3, dummy,
+    creact, v0, inv, wx, wyu, wyl, wzu, wzl, cinv, cwx, cwyu, cwyl, cwzu, cwzl, zs, sums, got1, got2, got3, dummy,
     end_zs, end_pack, end_halo, end_x, end_y, end_z, end_rs, send_sem, recv_sem, far_sem,
 ):
     nx, ny, nz = sizes
@@ -280,88 +280,115 @@
             slabs.append(jnp.concatenate([mid, jnp.concatenate(side, axis=1)], axis=0))
         return slabs
 
+    def is_own(i):
+        return 5 <= i < 9
+
+    def narrow(slab, i):
+        return slab if is_own(i) else fold_rows(slab)
+
+    def put(ref, i, value, whole):
+        if whole:
+            ref[i] = value
+        else:
+            ref[i, 0:8] = value[0:8]
+
     def coefficients():
-        face_x = [face_terms(mean_x[i], box_u[i + 1] - box_u[i]) for i in range(13)]
+        u16 = [fold_rows(box_u[i]) if is_own(i) else box_u[i, 0:16] for i in range(14)]
+        face_x = [face_terms(mean_x[i], u16[i + 1] - u16[i]) for i in range(13)]
         cface = []
         for j in range(7):
             cface.append(plane_sum(face_x[2 * j][1]))
             if 1 <= j < 6:
-                cwx[j - 1] = fold_rows(cface[j])
+                put(cwx, j - 1, cface[j], 1 < j < 5)
         for i in range(7):
-            wx[i] = fold_rows(face_x[i + 3][1])
+            put(wx, i, face_x[i + 3][1], 0 < i < 6)
+        odd_row = lax.rem(index_of((16, 2 * LINE), 0), 2) == 1
+        odd_lane = lax.rem(index_of((16, 2 * LINE), 1), 2) == 1
         for c in range(6):
-            pair_y, pair_z, pair_r = None, None, None
+            pairs = None
             for half in range(2):
                 i = 2 * c + half
-                u = box_u[i + 1]
-                re = react[i]
-                flux_y, w_y = face_terms(mean_y[i], up(u, 0) - u)
+                u, re = u16[i + 1], react[i]
+                if is_own(i + 1):
+                    tall = box_u[i + 1]
+                    flux, w = face_terms(mean_y[i], up(tall, 0) - tall)
+                    flux_y, w_y = fold_rows(flux), fold_rows(w)
+                    low_flux_y, low_y = fold_rows(down(flux, 0)), fold_rows(down(w, 0))
+                else:
+                    flux_y, w_y = face_terms(mean_y[i, 0:16], up(u, 0) - u)
+                    low_flux_y, low_y = down(flux_y, 0), down(w_y, 0)
                 flux_z, w_z = face_terms(mean_z[i], up(u, 1) - u)
-                low_y, low_z = down(w_y, 0), down(w_z, 1)
+                low_z = down(w_z, 1)
                 force = (
                     src[i]
                     - re * u
                     + (face_x[i + 1][0] - face_x[i][0])
-                    + (flux_y - down(flux_y, 0))
+                    + (flux_y - low_flux_y)
                     + (flux_z - down(flux_z, 1))
                 )
-                v0[i] = fold_rows(force)
+                put(v0, i, force, 2 <= i < 10)
                 if 2 <= i < 10:
                     diagonal = re + face_x[i + 1][1] + face_x[i][1] + w_y + low_y + w_z + low_z
-                    inv[i - 2] = fold_rows(1.0 / diagonal)
+                    put(inv, i - 2, 1.0 / diagonal, 3 <= i < 9)
                 if 3 <= i < 9:
-                    wyu[i - 3] = fold_rows(w_y)
-                    wyl[i - 3] = fold_rows(low_y)
-                    wzu[i - 3] = fold_rows(w_z)
-                    wzl[i - 3] = fold_rows(low_z)
-                pair_y = w_y if half == 0 else pair_y + w_y
-                pair_z = w_z if half == 0 else pair_z + w_z
-                pair_r = re if half == 0 else pair_r + re
-            odd_row = lax.rem(index_of((24, 2 * LINE), 0), 2) == 1
-            odd_lane = lax.rem(index_of((24, 2 * LINE), 1), 2) == 1
+                    for ref, weight in ((wyu, w_y), (wyl, low_y), (wzu, w_z), (wzl, low_z)):
+                        put(ref, i - 3, weight, 4 <= i < 8)
+                now = (w_y, low_y, w_z)
+                pairs = now if half == 0 else tuple(one + two for one, two in zip(pairs, now))
+            pair_y, pair_low, pair_z = pairs
             sum_y = pair_sum(jnp.where(odd_row, pair_y, up(pair_y, 0)), 1)
             sum_z = pair_sum(jnp.where(odd_lane, pair_z, up(pair_z, 1)), 0)
-            low_y, low_z = pltpu.roll(sum_y, 2, 0), pltpu.roll(sum_z, 2, 1)
-            diagonal = plane_sum(pair_r) + cface[c] + cface[c + 1] + sum_y + low_y + sum_z + low_z
-            cinv[c] = fold_rows(1.0 / diagonal)
+            if c in (2, 3):
+                low_y = pair_sum(jnp.where(odd_row, down(pair_low, 0), pair_low), 1)
+            else:
+                low_y = pltpu.roll(sum_y, 2, 0)
+            low_z = pltpu.roll(sum_z, 2, 1)
+            diagonal = creact[c] + cface[c] + cface[c + 1] + sum_y + low_y + sum_z + low_z
+            put(cinv, c, 1.0 / diagonal, 1 <= c < 5)
             if 1 <= c < 5:
-                cwyu[c - 1] = fold_rows(sum_y)
-                cwyl[c - 1] = fold_rows(low_y)
-                cwzu[c - 1] = fold_rows(sum_z)
-                cwzl[c - 1] = fold_rows(low_z)
+                for ref, weight in ((cwyu, sum_y), (cwyl, low_y), (cwzu, sum_z), (cwzl, low_z)):
+                    put(ref, c - 1, weight, 2 <= c < 4)
 
     def precondition(v, j):
-        own = [inv[i] * v[i + 2] for i in range(8)]
-        coarse = [cinv[c] * plane_sum(v[2 * c] + v[2 * c + 1]) for c in range(6)]
+        def part(whole):
+            return slice(0, 16) if whole else slice(0, 8)
+
+        own = [inv[i, part(0 < i < 7)] * v[i + 2][part(0 < i < 7)] for i in range(8)]
+        coarse = []
+        for c in range(6):
+            rows = part(1 <= c < 5)
+            coarse.append(cinv[c, rows] * plane_sum(v[2 * c][rows] + v[2 * c + 1][rows]))
         coarse_z = []
         for c in range(4):
-            q = coarse[c + 1]
+            q, rows = coarse[c + 1], part(1 <= c < 3)
             near = (
-                cwx[c] * coarse[c]
-                + cwx[c + 1] * coarse[c + 2]
-                + cwyu[c] * pltpu.roll(q, 14, 0)
-                + cwyl[c] * pltpu.roll(q, 2, 0)
-                + cwzu[c] * pltpu.roll(q, 2 * LINE - 2, 1)
-                + cwzl[c] * pltpu.roll(q, 2, 1)
+                cwx[c, rows] * coarse[c][rows]
+                + cwx[c + 1, rows] * coarse[c + 2][rows]
+                + cwyu[c, rows] * pltpu.roll(q, 14, 0)[rows]
+                + cwyl[c, rows] * pltpu.roll(q, 2, 0)[rows]
+                + cwzu[c, rows] * pltpu.roll(q[rows], 2 * LINE - 2, 1)
+                + cwzl[c, rows] * pltpu.roll(q[rows], 2, 1)
             )
-            coarse_z.append(COARSE_OWN * q + COARSE_NEAR * (cinv[c + 1] * near))
+            coarse_z.append(COARSE_OWN * q[rows] + COARSE_NEAR * (cinv[c + 1, rows] * near))
         for i in range(6):
-            q = own[i + 1]
+            q, rows = own[i + 1], part(0 < i < 5)
             near = (
-                wx[i] * own[i]
-                + wx[i + 1] * own[i + 2]
-                + wyu[i] * up(q, 0)
-                + wyl[i] * down(q, 0)
-                + wzu[i] * up(q, 1)
-                + wzl[i] * down(q, 1)
+                wx[i, rows] * own[i][rows]
+                + wx[i + 1, rows] * own[i + 2][rows]
+                + wyu[i, rows] * up(q, 0)[rows]
+                + wyl[i, rows] * down(q, 0)[rows]
+                + wzu[i, rows] * up(q[rows], 1)
+                + wzl[i, rows] * down(q[rows], 1)
             )
-            zs[j, i] = FINE_OWN * q + FINE_NEAR * (inv[i + 1] * near) + coarse_z[(i + 1) // 2]
+            zs[j, i, rows] = (
+                FINE_OWN * q[rows] + FINE_NEAR * (inv[i + 1, rows] * near) + coarse_z[(i + 1) // 2][rows]
+            )
 
     def image(j, s):
         i = s + 1
         tall = zs[j, i]
         here = tall[0:8]
-        total = react[i + 3, 8:16] * here
+        total = react[i + 3, 0:8] * here
         for weight, other in (
             (wx[i, 0:8], zs[j, i - 1, 0:8]),
             (wx[i + 1, 0:8], zs[j, i + 1, 0:8]),
@@ -461,17 +488,33 @@
     receive(count, 0)
     for other in far_ones:
         pl.semaphore_signal(far_sem, inc=1, device_id=other, device_id_type=MESH)
+    def put_box(i, value):
+        if is_own(i):
+            box_u[i] = value
+        else:
+            box_u[i, 0:16] = value
+
+    def get_box(i):
+        return box_u[i] if is_own(i) else box_u[i, 0:16]
+
+    k_slabs = []
     for i in range(14):
-        box_u[i] = wide_slab(raw0, corner0, zed0, far0, 0, i)
-    k_slabs = [wide_slab(raw0, corner0, zed0, far0, 1, i) for i in range(14)]
+        put_box(i, narrow(wide_slab(raw0, corner0, zed0, far0, 0, i), i))
+        k_slabs.append(narrow(wide_slab(raw0, corner0, zed0, far0, 1, i), i))
+    k16 = [fold_rows(k_slabs[i]) if is_own(i) else k_slabs[i] for i in range(14)]
     for i in range(13):
-        mean_x[i] = mean_of(k_slabs[i], k_slabs[i + 1])
+        mean_x[i] = mean_of(k16[i], k16[i + 1])
     for i in range(12):
         k = k_slabs[i + 1]
-        mean_y[i] = mean_of(k, up(k, 0))
-        mean_z[i] = mean_of(k, up(k, 1))
-        react[i] = wide_slab(raw0, corner0, zed0, far0, 2, i + 1, True)
-        src[i] = wide_slab(raw0, corner0, zed0, far0, 3, i + 1, True)
+        if is_own(i + 1):
+            mean_y[i] = mean_of(k, up(k, 0))
+        else:
+            mean_y[i, 0:16] = mean_of(k, up(k, 0))
+        mean_z[i] = mean_of(k16[i + 1], up(k16[i + 1], 1))
+        react[i] = fold_rows(wide_slab(raw0, corner0, zed0, far0, 2, i + 1, True))
+        src[i] = fold_rows(wide_slab(raw0, corner0, zed0, far0, 3, i + 1, True))
+    for c in range(6):
+        creact[c] = plane_sum(react[2 * c] + react[2 * c + 1])
 
     own = (slice(0, 8), slice(0, LINE))
 
@@ -492,7 +535,7 @@
     def beside_v(newton, j):
         if newton == 0 and j == 0:
             for i in range(6):
-                zs[7, i] = fold_rows(k_slabs[i + 4])
+                zs[7, i] = k16[i + 4]
             give_field(7, 14)
         elif newton == 1:
             if j == 0:
@@ -518,7 +561,7 @@
     for newton in range(NEWTON):
         coefficients()
         rows = []
-        v = [v0[i] for i in range(12)]
+        v = [v0[i] if 2 <= i < 10 else v0[i, 0:8] for i in range(12)]
         tiles = [slab[0:8] for slab in v[4:8]]
         for j in range(KRYLOV):
             at = 4 * newton + j
@@ -551,12 +594,12 @@
         if newton + 1 < NEWTON:
             receive(sum(counts), 1)
             for i in range(14):
-                total = box_u[i]
+                total = get_box(i)
                 for j in range(3):
-                    total = total + c[j] * wide_slab(raw_h, corner_h, zed_h, far_h, j, i)
-                box_u[i] = total
+                    total = total + c[j] * narrow(wide_slab(raw_h, corner_h, zed_h, far_h, j, i), i)
+                put_box(i, total)
                 if 4 <= i < 10:
-                    zs[3, i - 4] = fold_rows(total)
+                    zs[3, i - 4] = fold_rows(total) if is_own(i) else total
 
     last_r.wait()
     last_s.wait()
@@ -606,7 +649,7 @@
         vmem(4, 14, 24, LINE), vmem(2, 2, 4, 2, *tile), vmem(3, 3, 2, 2, *tile), vmem(2, 2, 2, *tile),
         vmem(3, 14, 24, LINE), vmem(2, 2, 3, 2, *tile), vmem(3, 3, 2, 2, *tile), vmem(2, 2, 2, *tile),
         vmem(4, 6, *tile), vmem(4, 4, 5, *tile), vmem(4, 2, 2, 3, *tile), vmem(2, 2, 2, *tile), vmem(2, 2, 4, 2, *tile), vmem(14, *full),
-        vmem(13, *full), vmem(12, *full), vmem(12, *full), vmem(12, *full), vmem(12, *full),
+        vmem(13, *half), vmem(12, *full), vmem(12, *half), vmem(12, *half), vmem(12, *half), vmem(6, *half),
         vmem(12, *half), vmem(8, *half), vmem(7, *half), vmem(6, *half), vmem(6, *half), vmem(6, *half), vmem(6, *half),
         vmem(6, *half), vmem(5, *half), vmem(4, *half), vmem(4, *half), vmem(4, *half), vmem(4, *half),
         vmem(8, 6, *half), vmem(2, 3, 1, LINE), vmem(2, 1, 1, LINE), vmem(2, plane - 1, 1, LINE), vmem(2, line - 1, 1, LINE),

time: 79.3 us -> 77.7 us (0.980)
  Pallas kernels: 77 us -> 75.4 us
    pallas_call x1, Pallas kernels: 77 us -> 75.4 us  [local(): pl.pallas_call(functools.partial(kernel, sizes), out_shape=jax.ShapeDtype...]
where the time goes in v7:
time: 77.7 us; the launch traced here: 77.4 us
  Pallas kernels  75.4 us (97%)
  local copies, waits for them, and re-layouts  1.35 us (2%)
    pallas_call x1, Pallas kernels, local(): pl.pallas_call(functools.partial(kernel, sizes), out_shape=jax.ShapeDtype...  75.4 us

profile of v7, /device:TPU:1, one launch (start us, length us, event | category | flops | bytes accessed | tf_op | source)
XLA Modules:
  0.0 77.4 jit_solution(14317507553825376064)
XLA Ops:
  0.6 75.4 %shard_map.59 = f32[2,4,8,128]{3,2,1,0:T(8,128)} custom-call(f32[4,8,128]{2,1,0:T(8,128)} %u_ref.1, f32[4,8,128]{2,1,0:T(8,128)} %k_ref.1, f32[4,8,128]{2,1,0:T(8,128)} %r_ref.1, f32[4,8,128]{2,1,0:T(8,128)} %s_ref.1), custom_call_target="tpu_custom_call" | custom-call | tf_op jit(solution)/shard_map/pallas_call | solution.py:661
  76.1 1.3 %slice_bitcast_fusion = (f32[4,8,128]{2,1,0:T(8,128)}, f32[4,8,128]{2,1,0:T(8,128)}) fusion(f32[2,4,8,128]{3,2,1,0:T(8,128)} %shard_map.59), kind=kLoop, calls=%fused_computation | loop fusion | bytes 65536 | tf_op jit(solution)/shard_map/squeeze | solution.py:671

commit v8 on v7

--- a/solution.py
+++ b/solution.py
@@ -73,7 +73,7 @@
 
 def kernel(
     sizes, u_ref, k_ref, r_ref, s_ref, out,
-    raw0, corner0, zed0, far0, raw_h, corner_h, zed_h, far_h, v_out, v_face, v_edge, pack, corner_pack, box_u, mean_x, mean_y, mean_z, react, src,
+    raw0, corner0, zed0, far0, raw_h, corner_h, zed_h, far_h, v_out, v_face, v_edge, pack, corner_pack, box_u, box_z, mean_x, mean_y, mean_z, react, src,
     creact, v0, inv, wx, wyu, wyl, wzu, wzl, cinv, cwx, cwyu, cwyl, cwzu, cwzl, zs, sums, got1, got2, got3, dummy,
     end_zs, end_pack, end_halo, end_x, end_y, end_z, end_rs, send_sem, recv_sem, far_sem,
 ):
@@ -90,18 +90,19 @@
         return ((x // 4) * 4 + y, lax.rem(x, 4), lax.rem(mz + dz + nz, nz))
 
     core_line = [(mx, my, (mz // 2) * 2 + 1 - lax.rem(mz, 2))]
-    plane = 4 * (nz // 2)
-    here = lax.rem(mx, 4) * (nz // 2) + mz // 2
+    def around(step, size):
+        return min(step, size - step)
+
+    chips = nz // 2
     plane_line = []
-    for step in range(1, plane):
-        there = lax.rem(here + step, plane)
-        plane_line.append(
-            ((mx // 4) * 4 + there // (nz // 2), my, lax.rem(there, nz // 2) * 2 + lax.rem(mz, 2))
-        )
+    steps = [(dy, dx) for dy in range(4) for dx in range(chips)][1:]
+    for dy, dx in sorted(steps, key=lambda d: -around(d[0], 4) - around(d[1], chips)):
+        x = lax.rem(mz // 2 + dx, chips)
+        plane_line.append(((mx // 4) * 4 + lax.rem(mx + dy, 4), my, x * 2 + lax.rem(mz, 2)))
     line = (nx // 4) * ny
     at = (mx // 4) * ny + my
     long_line = []
-    for step in range(1, line):
+    for step in sorted(range(1, line), key=lambda d: -around(d, line)):
         there = lax.rem(at + step, line)
         long_line.append(((there // ny) * 4 + lax.rem(mx, 4), lax.rem(there, ny), mz))
 
@@ -400,14 +401,18 @@
             total = total + weight * (here - other)
         return total
 
-    def global_sum(rows, which, between):
+    group_of = lane // 16
+
+    def gather(total, moments):
+        for n, tile in moments:
+            for shift in (64, 32, 16):
+                tile = tile + pltpu.roll(tile, shift, 1)
+            total = total + jnp.where(group_of == n, tile, 0.0)
+        return total
+
+    def global_sum(tile, which, beside):
         group = index_of((1, LINE), 1) // 16
-        mixed = jnp.zeros((1, LINE), jnp.float32)
-        for n, row in enumerate(rows):
-            row = jnp.sum(row, axis=0, keepdims=True)
-            for shift in (64, 32, 16):
-                row = row + pltpu.roll(row, shift, 1)
-            mixed = jnp.where(group == n, row, mixed)
+        mixed = jnp.sum(tile, axis=0, keepdims=True)
         phases = ((core_line, got1), (plane_line, got2), (long_line, got3))
         for phase, (partners, got) in enumerate(phases):
             if phase == 1 and which == 0:
@@ -416,8 +421,7 @@
             slot = 6 + 3 * which + phase
             for n, partner in enumerate(partners):
                 send(sums.at[which, phase], got.at[which, n], slot, partner)
-            if phase == 1:
-                between()
+            beside(phase)
             part = got.at[which]
             pltpu.make_async_copy(part, part, recv_sem.at[slot]).wait()
             mixed = mixed + jnp.sum(got[which], axis=0)
@@ -560,43 +564,59 @@
 
     for newton in range(NEWTON):
         coefficients()
-        rows = []
+        sofar = []
+        moments = []
         v = [v0[i] if 2 <= i < 10 else v0[i, 0:8] for i in range(12)]
         tiles = [slab[0:8] for slab in v[4:8]]
         for j in range(KRYLOV):
             at = 4 * newton + j
             precondition(v, at)
             z_tiles = [zs[(at, s + 1) + own] for s in range(4)]
-            rows.append(total_of(tiles, z_tiles))
+            moments.append((2 * j, total_of(tiles, z_tiles)))
             if newton + 1 < NEWTON:
                 for s in range(4):
                     raw_h[j, 5 + s, 8:16] = z_tiles[s]
             tiles = [SCALE * image(at, s) - SHIFT * tiles[s] for s in range(4)]
-            rows.append(total_of(tiles, z_tiles))
+            moments.append((2 * j + 1, total_of(tiles, z_tiles)))
             if j + 1 < KRYLOV:
-                v = exchange_v(tiles, 2 * newton + j, functools.partial(beside_v, newton, j))
+
+                def meanwhile(newton=newton, j=j, moments=moments):
+                    sofar.append(gather(sofar[-1] if j else nothing, moments))
+                    beside_v(newton, j)
+
+                v = exchange_v(tiles, 2 * newton + j, meanwhile)
+                moments = []
 
         counts = []
 
-        def beside(newton=newton, counts=counts):
-            if newton + 1 < NEWTON:
+        def beside(phase, newton=newton, counts=counts):
+            if phase == 1 and newton + 1 < NEWTON:
                 pack_corners(raw_h, 1, 0, 3)
                 counts.append(exchange_wide(raw_h, corner_h, 1, 0, 3, True, 1))
                 pack_z([raw_h[f, 5 + s, 8:16] for f in range(2) for s in range(4)], 1, 0)
                 pack_z([raw_h[2, 5 + s, 8:16] for s in range(4)], 1, 1)
                 counts.append(exchange_far(raw_h, far_h, 1, 3, 1))
                 counts.append(exchange_z(zed_h, 1, 1))
-            else:
+            elif phase == 1:
                 give_field(6, 13)
                 end_means()
-
-        c = solve(global_sum(rows, newton, beside))
+            elif phase == 2 and newton + 1 < NEWTON:
+                receive(sum(counts), 1)
+                for j in range(3):
+                    for i in range(14):
+                        slab = narrow(wide_slab(raw_h, corner_h, zed_h, far_h, j, i), i)
+                        if is_own(i):
+                            box_z[j, i] = slab
+                        else:
+                            box_z[j, i, 0:16] = slab
+
+        c = solve(global_sum(gather(sofar[-1], moments), newton, beside))
         if newton + 1 < NEWTON:
-            receive(sum(counts), 1)
             for i in range(14):
+                rows = slice(0, 24 if is_own(i) else 16)
                 total = get_box(i)
                 for j in range(3):
-                    total = total + c[j] * narrow(wide_slab(raw_h, corner_h, zed_h, far_h, j, i), i)
+                    total = total + c[j] * box_z[j, i, rows]
                 put_box(i, total)
                 if 4 <= i < 10:
                     zs[3, i - 4] = fold_rows(total) if is_own(i) else total
@@ -648,7 +668,7 @@
     scratch = [
         vmem(4, 14, 24, LINE), vmem(2, 2, 4, 2, *tile), vmem(3, 3, 2, 2, *tile), vmem(2, 2, 2, *tile),
         vmem(3, 14, 24, LINE), vmem(2, 2, 3, 2, *tile), vmem(3, 3, 2, 2, *tile), vmem(2, 2, 2, *tile),
-        vmem(4, 6, *tile), vmem(4, 4, 5, *tile), vmem(4, 2, 2, 3, *tile), vmem(2, 2, 2, *tile), vmem(2, 2, 4, 2, *tile), vmem(14, *full),
+        vmem(4, 6, *tile), vmem(4, 4, 5, *tile), vmem(4, 2, 2, 3, *tile), vmem(2, 2, 2, *tile), vmem(2, 2, 4, 2, *tile), vmem(14, *full), vmem(3, 14, *full),
         vmem(13, *half), vmem(12, *full), vmem(12, *half), vmem(12, *half), vmem(12, *half), vmem(6, *half),
         vmem(12, *half), vmem(8, *half), vmem(7, *half), vmem(6, *half), vmem(6, *half), vmem(6, *half), vmem(6, *half),
         vmem(6, *half), vmem(5, *half), vmem(4, *half), vmem(4, *half), vmem(4, *half), vmem(4, *half),

time: 77.7 us -> 76.8 us (0.988)
  Pallas kernels: 75.4 us -> 74.5 us
    pallas_call x1, Pallas kernels: 75.4 us -> 74.5 us  [local(): pl.pallas_call(functools.partial(kernel, sizes), out_shape=jax.ShapeDtype...]
where the time goes in v8:
time: 76.8 us; the launch traced here: 76.5 us
  Pallas kernels  74.5 us (97%)
  local copies, waits for them, and re-layouts  1.35 us (2%)
    pallas_call x1, Pallas kernels, local(): pl.pallas_call(functools.partial(kernel, sizes), out_shape=jax.ShapeDtype...  74.5 us

profile of v8, /device:TPU:1, one launch (start us, length us, event | category | flops | bytes accessed | tf_op | source)
XLA Modules:
  0.0 76.5 jit_solution(2265584155130157563)
XLA Ops:
  0.6 74.5 %shard_map.59 = f32[2,4,8,128]{3,2,1,0:T(8,128)} custom-call(f32[4,8,128]{2,1,0:T(8,128)} %u_ref.1, f32[4,8,128]{2,1,0:T(8,128)} %k_ref.1, f32[4,8,128]{2,1,0:T(8,128)} %r_ref.1, f32[4,8,128]{2,1,0:T(8,128)} %s_ref.1), custom_call_target="tpu_custom_call" | custom-call | tf_op jit(solution)/shard_map/pallas_call | solution.py:681
  75.2 1.3 %slice_bitcast_fusion = (f32[4,8,128]{2,1,0:T(8,128)}, f32[4,8,128]{2,1,0:T(8,128)}) fusion(f32[2,4,8,128]{3,2,1,0:T(8,128)} %shard_map.59), kind=kLoop, calls=%fused_computation | loop fusion | bytes 65536 | tf_op jit(solution)/shard_map/squeeze | solution.py:691

commit v9 on v8

--- a/solution.py
+++ b/solution.py
@@ -73,7 +73,7 @@
 
 def kernel(
     sizes, u_ref, k_ref, r_ref, s_ref, out,
-    raw0, corner0, zed0, far0, raw_h, corner_h, zed_h, far_h, v_out, v_face, v_edge, pack, corner_pack, box_u, box_z, mean_x, mean_y, mean_z, react, src,
+    raw0, corner0, zed0, far0, raw_h, corner_h, zed_h, far_h, v_out_x, v_out_y, v_face_x, v_face_y, v_edge, pack, corner_pack, box_u, box_z, mean_x, mean_y, mean_z, react, src,
     creact, v0, inv, wx, wyu, wyl, wzu, wzl, cinv, cwx, cwyu, cwyl, cwzu, cwzl, zs, sums, got1, got2, got3, dummy,
     end_zs, end_pack, end_halo, end_x, end_y, end_z, end_rs, send_sem, recv_sem, far_sem,
 ):
@@ -234,51 +234,73 @@
 
     def exchange_v(tiles, e, between):
         slot = 2 + e
+        low_rows = index_of((ROWS, LINE), 0) < 4
+        mains = [tile[:, 0:LINE] for tile in tiles]
         packed = nothing
         for s in range(4):
-            v_out[e, 1 + s] = tiles[s][:, 0:LINE]
             part = pltpu.roll(tiles[s][:, LINE : 2 * LINE], 16 * s + 8, 1)
             packed = jnp.where(lane // 16 == s, part, packed)
-        v_out[e, 0] = packed
-        v_out[e, 5] = packed
+        for pair in range(2):
+            one, two = mains[2 * pair], pltpu.roll(mains[2 * pair + 1], 4, 0)
+            v_out_y[e, 1, 1 + pair] = jnp.where(low_rows, two, one)
+            v_out_y[e, 0, 1 + pair] = jnp.where(low_rows, one, two)
+        for way in range(2):
+            v_out_y[e, way, 0] = packed
+            v_out_y[e, way, 3] = packed
+        for n, tile in enumerate(
+            (mains[0] + mains[1], mains[2], mains[3], packed, mains[0], mains[1], mains[2] + mains[3])
+        ):
+            v_out_x[e, n] = tile
         for dx, dy in CORNERS:
             send(
-                v_out.at[e, pl.ds(3 if dx > 0 else 0, 3)],
+                v_out_y.at[e, (1 + dy) // 2, pl.ds(1 + dx, 2)],
                 v_edge.at[e, (1 - dx) // 2, (1 - dy) // 2],
                 slot,
                 block_at(dx, dy, 0),
             )
-        for n, (dx, dy) in enumerate(CROSS[1:]):
-            send(v_out.at[e, pl.ds(1, 5)], v_face.at[e, n], slot, block_at(dx, dy, 0))
+        for n, dx in enumerate((1, -1)):
+            send(v_out_x.at[e, pl.ds(3 * n, 4)], v_face_x.at[e, n], slot, block_at(dx, 0, 0))
+        for n, dy in enumerate((1, -1)):
+            send(v_out_y.at[e, 1 - n, pl.ds(1, 3)], v_face_y.at[e, n], slot, block_at(0, dy, 0))
         between()
-        receive(12 + 20, slot)
-        row = index_of((ROWS, LINE), 0)
+        receive(8 + 8 + 6, slot)
 
         def spread(zeds, s):
             return pltpu.roll(zeds, LINE - 8 - 16 * s, 1)
+
+        def both(low, high, s):
+            if s % 2 == 0:
+                return jnp.where(low_rows, high, low)
+            return pltpu.roll(jnp.where(low_rows, low, high), 4, 0)
 
         slabs = []
         for i in range(12):
             column, s = divmod(i, 4)
             if column == 1:
                 mid = tiles[s]
+                low, high = v_face_y[e, 0], v_face_y[e, 1]
                 side = [
-                    jnp.where(row < 4, v_face[e, 3, s], v_face[e, 2, s]),
-                    jnp.where(row < 4, spread(v_face[e, 3, 4], s), spread(v_face[e, 2, 4], s)),
+                    both(low[s // 2], high[s // 2], s),
+                    spread(jnp.where(low_rows, high[2], low[2]), s),
                 ]
+                slabs.append(jnp.concatenate([mid, jnp.concatenate(side, axis=1)], axis=0))
+                continue
+            face = column // 2
+            got = v_face_x[e, face]
+            z_at, z_edge, one_edge = (3, 1, 0) if face == 0 else (0, 0, 1)
+            if 2 <= i < 10:
+                mid = jnp.concatenate([got[s - 1 if face == 0 else s + 1], spread(got[z_at], s)], axis=1)
+                low, high = v_edge[e, face, 0], v_edge[e, face, 1]
+                side = [
+                    both(low[one_edge], high[one_edge], s),
+                    spread(jnp.where(low_rows, high[z_edge], low[z_edge]), s),
+                ]
+                slabs.append(jnp.concatenate([mid, jnp.concatenate(side, axis=1)], axis=0))
+            elif i in (0, 10):
+                two = spread(got[z_at], s) + spread(got[z_at], s + 1)
+                slabs.append(jnp.concatenate([got[0 if face == 0 else 3], two], axis=1))
             else:
-                face = 0 if column == 0 else 1
-                mid = jnp.concatenate([v_face[e, face, s], spread(v_face[e, face, 4], s)], axis=1)
-                side = [nothing, nothing]
-                if 2 <= i < 10:
-                    at = s - 2 if column == 0 else s + 1
-                    z_at = 2 if column == 0 else 0
-                    low, high = v_edge.at[e, face, 0], v_edge.at[e, face, 1]
-                    side = [
-                        jnp.where(row < 4, high[at], low[at]),
-                        jnp.where(row < 4, spread(high[z_at], s), spread(low[z_at], s)),
-                    ]
-            slabs.append(jnp.concatenate([mid, jnp.concatenate(side, axis=1)], axis=0))
+                slabs.append(None)
         return slabs
 
     def is_own(i):
@@ -358,7 +380,8 @@
         coarse = []
         for c in range(6):
             rows = part(1 <= c < 5)
-            coarse.append(cinv[c, rows] * plane_sum(v[2 * c][rows] + v[2 * c + 1][rows]))
+            pair = v[2 * c][rows] if v[2 * c + 1] is None else v[2 * c][rows] + v[2 * c + 1][rows]
+            coarse.append(cinv[c, rows] * plane_sum(pair))
         coarse_z = []
         for c in range(4):
             q, rows = coarse[c + 1], part(1 <= c < 3)
@@ -668,7 +691,7 @@
     scratch = [
         vmem(4, 14, 24, LINE), vmem(2, 2, 4, 2, *tile), vmem(3, 3, 2, 2, *tile), vmem(2, 2, 2, *tile),
         vmem(3, 14, 24, LINE), vmem(2, 2, 3, 2, *tile), vmem(3, 3, 2, 2, *tile), vmem(2, 2, 2, *tile),
-        vmem(4, 6, *tile), vmem(4, 4, 5, *tile), vmem(4, 2, 2, 3, *tile), vmem(2, 2, 2, *tile), vmem(2, 2, 4, 2, *tile), vmem(14, *full), vmem(3, 14, *full),
+        vmem(4, 7, *tile), vmem(4, 2, 4, *tile), vmem(4, 2, 4, *tile), vmem(4, 2, 3, *tile), vmem(4, 2, 2, 2, *tile), vmem(2, 2, 2, *tile), vmem(2, 2, 4, 2, *tile), vmem(14, *full), vmem(3, 14, *full),
         vmem(13, *half), vmem(12, *full), vmem(12, *half), vmem(12, *half), vmem(12, *half), vmem(6, *half),
         vmem(12, *half), vmem(8, *half), vmem(7, *half), vmem(6, *half), vmem(6, *half), vmem(6, *half), vmem(6, *half),
         vmem(6, *half), vmem(5, *half), vmem(4, *half), vmem(4, *half), vmem(4, *half), vmem(4, *half),

time: 76.8 us -> 76.5 us (level)
  no operation moved by 1% of the time
where the time goes in v9:
time: 76.5 us; the launch traced here: 76.2 us
  Pallas kernels  74.3 us (97%)
  local copies, waits for them, and re-layouts  1.35 us (2%)
    pallas_call x1, Pallas kernels, local(): pl.pallas_call(functools.partial(kernel, sizes), out_shape=jax.ShapeDtype...  74.3 us

profile of v9, /device:TPU:1, one launch (start us, length us, event | category | flops | bytes accessed | tf_op | source)
XLA Modules:
  0.0 76.2 jit_solution(2814493869338771141)
XLA Ops:
  0.6 74.3 %shard_map.59 = f32[2,4,8,128]{3,2,1,0:T(8,128)} custom-call(f32[4,8,128]{2,1,0:T(8,128)} %u_ref.1, f32[4,8,128]{2,1,0:T(8,128)} %k_ref.1, f32[4,8,128]{2,1,0:T(8,128)} %r_ref.1, f32[4,8,128]{2,1,0:T(8,128)} %s_ref.1), custom_call_target="tpu_custom_call" | custom-call | tf_op jit(solution)/shard_map/pallas_call | solution.py:704
  74.9 1.3 %slice_bitcast_fusion = (f32[4,8,128]{2,1,0:T(8,128)}, f32[4,8,128]{2,1,0:T(8,128)}) fusion(f32[2,4,8,128]{3,2,1,0:T(8,128)} %shard_map.59), kind=kLoop, calls=%fused_computation | loop fusion | bytes 65536 | tf_op jit(solution)/shard_map/squeeze | solution.py:714

commit v10 on v9

--- a/solution.py
+++ b/solution.py
@@ -74,7 +74,7 @@
 def kernel(
     sizes, u_ref, k_ref, r_ref, s_ref, out,
     raw0, corner0, zed0, far0, raw_h, corner_h, zed_h, far_h, v_out_x, v_out_y, v_face_x, v_face_y, v_edge, pack, corner_pack, box_u, box_z, mean_x, mean_y, mean_z, react, src,
-    creact, v0, inv, wx, wyu, wyl, wzu, wzl, cinv, cwx, cwyu, cwyl, cwzu, cwzl, zs, sums, got1, got2, got3, dummy,
+    creact, v0, inv, wx, wyu, wyl, wzu, wzl, cinv, cwx, cwyu, cwyl, cwzu, cwzl, zs, sums, got2, got3, dummy,
     end_zs, end_pack, end_halo, end_x, end_y, end_z, end_rs, send_sem, recv_sem, far_sem,
 ):
     nx, ny, nz = sizes
@@ -89,16 +89,15 @@
         x, y = lax.rem(bx + dx + nx, nx), lax.rem(by + dy + ny, ny)
         return ((x // 4) * 4 + y, lax.rem(x, 4), lax.rem(mz + dz + nz, nz))
 
-    core_line = [(mx, my, (mz // 2) * 2 + 1 - lax.rem(mz, 2))]
     def around(step, size):
         return min(step, size - step)
 
     chips = nz // 2
     plane_line = []
-    steps = [(dy, dx) for dy in range(4) for dx in range(chips)][1:]
-    for dy, dx in sorted(steps, key=lambda d: -around(d[0], 4) - around(d[1], chips)):
+    steps = [(dy, dx, dc) for dy in range(4) for dx in range(chips) for dc in range(2)][1:]
+    for dy, dx, dc in sorted(steps, key=lambda d: -around(d[0], 4) - around(d[1], chips)):
         x = lax.rem(mz // 2 + dx, chips)
-        plane_line.append(((mx // 4) * 4 + lax.rem(mx + dy, 4), my, x * 2 + lax.rem(mz, 2)))
+        plane_line.append(((mx // 4) * 4 + lax.rem(mx + dy, 4), my, x * 2 + lax.rem(mz + dc, 2)))
     line = (nx // 4) * ny
     at = (mx // 4) * ny + my
     long_line = []
@@ -436,8 +435,7 @@
     def global_sum(tile, which, beside):
         group = index_of((1, LINE), 1) // 16
         mixed = jnp.sum(tile, axis=0, keepdims=True)
-        phases = ((core_line, got1), (plane_line, got2), (long_line, got3))
-        for phase, (partners, got) in enumerate(phases):
+        for phase, partners, got in ((1, plane_line, got2), (2, long_line, got3)):
             if phase == 1 and which == 0:
                 pl.semaphore_wait(far_sem, 4)
             sums[which, phase] = mixed
@@ -681,7 +679,7 @@
 
 def local(sizes, state, conductivity, reaction, source):
     nx, ny, nz = sizes
-    plane, line = 4 * (nz // 2), (nx // 4) * ny
+    plane, line = 4 * nz, (nx // 4) * ny
 
     def vmem(*shape):
         return pltpu.VMEM(shape, jnp.float32)
@@ -695,7 +693,7 @@
         vmem(13, *half), vmem(12, *full), vmem(12, *half), vmem(12, *half), vmem(12, *half), vmem(6, *half),
         vmem(12, *half), vmem(8, *half), vmem(7, *half), vmem(6, *half), vmem(6, *half), vmem(6, *half), vmem(6, *half),
         vmem(6, *half), vmem(5, *half), vmem(4, *half), vmem(4, *half), vmem(4, *half), vmem(4, *half),
-        vmem(8, 6, *half), vmem(2, 3, 1, LINE), vmem(2, 1, 1, LINE), vmem(2, plane - 1, 1, LINE), vmem(2, line - 1, 1, LINE),
+        vmem(8, 6, *half), vmem(2, 3, 1, LINE), vmem(2, plane - 1, 1, LINE), vmem(2, line - 1, 1, LINE),
         vmem(160, *tile),
         vmem(5, 6, *tile), vmem(5, 2, *tile), vmem(5, 2, *tile), vmem(5, *tile), vmem(4, 16, LINE), vmem(4, ROWS, 2 * LINE), vmem(2, 4, *tile),
         pltpu.SemaphoreType.DMA((4,)), pltpu.SemaphoreType.DMA((16,)), pltpu.SemaphoreType.REGULAR,

time: 76.5 us -> 75.7 us (0.990)
  Pallas kernels: 74.3 us -> 73.5 us
    pallas_call x1, Pallas kernels: 74.3 us -> 73.5 us  [local(): pl.pallas_call(functools.partial(kernel, sizes), out_shape=jax.ShapeDtype...]
where the time goes in v10:
time: 75.7 us; the launch traced here: 75.4 us
  Pallas kernels  73.5 us (97%)
  local copies, waits for them, and re-layouts  1.35 us (2%)
    pallas_call x1, Pallas kernels, local(): pl.pallas_call(functools.partial(kernel, sizes), out_shape=jax.ShapeDtype...  73.5 us

profile of v10, /device:TPU:1, one launch (start us, length us, event | category | flops | bytes accessed | tf_op | source)
XLA Modules:
  0.0 75.4 jit_solution(795874679401646817)
XLA Ops:
  0.6 73.5 %shard_map.59 = f32[2,4,8,128]{3,2,1,0:T(8,128)} custom-call(f32[4,8,128]{2,1,0:T(8,128)} %u_ref.1, f32[4,8,128]{2,1,0:T(8,128)} %k_ref.1, f32[4,8,128]{2,1,0:T(8,128)} %r_ref.1, f32[4,8,128]{2,1,0:T(8,128)} %s_ref.1), custom_call_target="tpu_custom_call" | custom-call | tf_op jit(solution)/shard_map/pallas_call | solution.py:702
  74.1 1.3 %slice_bitcast_fusion = (f32[4,8,128]{2,1,0:T(8,128)}, f32[4,8,128]{2,1,0:T(8,128)}) fusion(f32[2,4,8,128]{3,2,1,0:T(8,128)} %shard_map.59), kind=kLoop, calls=%fused_computation | loop fusion | bytes 65536 | tf_op jit(solution)/shard_map/squeeze | solution.py:712
